TPU v7x, 128 devices: a whole 4x4x4 slice. The times are simulated.
128 devices in a mesh: chan: 64 (over z, y, x), row: 2 (over core).
Axes of the slice: x: 4, y: 4, z: 4, core: 2. Of those that a mesh axis runs over, the one named last changes fastest.
Arguments:
- generator: bfloat16 [64, 1280, 1280], P('chan', 'row'), may hold values from -0.25155765 to 0.25155765, as said below
- magnus_old: bfloat16 [64, 1280, 1280], P('chan', 'row'), may hold values from -0.25155765 to 0.25155765, as said below
- hamiltonian: bfloat16 [64, 1280, 1280], P('chan', 'row'), may hold values from -9 to 9, as said below
- chan_of_slot: int32 [64], P('chan'), may hold values from 0 to 63, each once
- chan_dims: int32 [64], replicated, may hold values from 160 to 1280, as said below
- pp_factor: float32 [64, 1280], replicated, may hold values from -1 to 1, as said below
- cc_factor: float32 [64, 1280], P('chan'), may hold values from -1 to 1, as said below
- send_table: int32 [64, 64, 3], P('chan'), may hold values from 0 to 160, as said below
- recv_table: int32 [64, 160], P('chan'), may hold values from 0 to 191, as said below
- pandya_weight: float32 [64, 160], P('chan'), may hold values from 0.5 to 2
Outputs:
- magnus_new: bfloat16 [64, 1280, 1280], P('chan', 'row')
- flowed: bfloat16 [64, 1280, 1280], P('chan', 'row')
Inputs may be any that keep to these rules, and one draw needn't show every extreme that they name: `generator`: antisymmetric in its last two dimensions. `magnus_old`: antisymmetric in its last two dimensions. `hamiltonian`: symmetric in its last two dimensions. `chan_dims`: live order of each channel; one channel has exactly 1280. `pp_factor`: every entry is -1, 0 or 1. `cc_factor`: every entry is -1, 0 or 1. send_table[p, d, l] is the local tile that group p sends to group d in slot l; 160 marks an empty slot; each local tile is sent exactly once; every group fills all 3 slots towards some peer. recv_table[d, v] = p * 3 + l names a filled slot of send_table[p, d, l]; every group receives exactly 160 tiles, each filled slot once.
All inputs are finite; a program needn't handle non-finite values.
Results may differ from a plain program's by a relative error of at most 0.0065.
Values may be sent and summed in bfloat16 or wider, within the bound.
A program may use at most 128 MiB of HBM per device.

v0:
```python
import jax
import jax.numpy as jnp
from jax import lax
from jax.sharding import PartitionSpec as P

TR = 40
COLT = 128


STEP_SIZE = 0.5


def cut_tiles(strip):
    slot_count, strip_rows, strip_width = strip.shape
    tile_grid = strip.reshape(slot_count, strip_rows // TR, TR, strip_width // COLT, COLT)
    return tile_grid.transpose(0, 1, 3, 2, 4).reshape(-1, TR, COLT)


def join_tiles(tile_stack, slot_count, strip_rows, strip_width):
    tile_grid = tile_stack.reshape(slot_count, strip_rows // TR, strip_width // COLT, TR, COLT)
    return tile_grid.transpose(0, 1, 3, 2, 4).reshape(slot_count, strip_rows, strip_width)


def contract(left_side, right_side):
    return jnp.einsum("sik,skj->sij", left_side, right_side, preferred_element_type=jnp.float32)


def fold_rows(left_side, row_piece):
    return contract(left_side, row_piece)


def per_device(
    generator,
    magnus_old,
    hamiltonian,
    chan_of_slot,
    chan_dims,
    pp_factor,
    cc_factor,
    send_table,
    recv_table,
    pandya_weight,
):
    slot_count, strip_rows, strip_width = generator.shape
    magnus_new = (
        magnus_old.astype(jnp.float32) + STEP_SIZE * generator.astype(jnp.float32)
    ).astype(jnp.bfloat16)
    channel_ids = jnp.arange(pp_factor.shape[0], dtype=jnp.int32)
    chosen = chan_of_slot[:, None] == channel_ids[None, :]
    limits = jnp.sum(jnp.where(chosen, chan_dims[None, :], 0), axis=1)
    factor_pp = jnp.dot(chosen.astype(jnp.float32), pp_factor, precision=lax.Precision.HIGHEST)
    row_ids = lax.axis_index("row") * strip_rows + jnp.arange(strip_rows, dtype=jnp.int32)
    col_ids = jnp.arange(strip_width, dtype=jnp.int32)
    live_mask = (row_ids[None, :, None] < limits[:, None, None]) & (
        col_ids[None, None, :] < limits[:, None, None]
    )
    zero_half = jnp.zeros((), jnp.bfloat16)
    magnus_live = jnp.where(live_mask, magnus_new, zero_half)
    hamilton_live = jnp.where(live_mask, hamiltonian, zero_half)
    send_order = send_table[0]
    recv_order = recv_table[0]
    tile_total = recv_order.shape[0]
    weights = pandya_weight[0][:, None, None]
    blank_tile = jnp.zeros((1, TR, COLT), jnp.bfloat16)
    outgoing_magnus = jnp.concatenate([cut_tiles(magnus_live), blank_tile])[send_order]
    outgoing_hamilton = jnp.concatenate([cut_tiles(hamilton_live), blank_tile])[send_order]
    arrived_magnus, arrived_hamilton = (
        lax.all_to_all(outgoing_magnus, "chan", split_axis=0, concat_axis=0, tiled=True),
        lax.all_to_all(outgoing_hamilton, "chan", split_axis=0, concat_axis=0, tiled=True),
    )

    def settle(arrived):
        picked = arrived.reshape(-1, TR, COLT)[recv_order]
        return join_tiles(
            (weights * picked.astype(jnp.float32)).astype(jnp.bfloat16),
            slot_count,
            strip_rows,
            strip_width,
        )

    magnus_cross = settle(arrived_magnus)
    hamilton_cross = settle(arrived_hamilton)
    scale_pp = factor_pp.astype(jnp.bfloat16)[:, None, :]
    scale_cc = cc_factor.astype(jnp.bfloat16)[:, None, :]
    forward_pp = fold_rows(
        magnus_live * scale_pp, lax.all_gather(hamilton_live, "row", axis=1, tiled=True)
    )
    magnus_full = lax.all_gather(magnus_live, "row", axis=1, tiled=True)
    backward_pp = contract(hamilton_live * scale_pp, magnus_full)
    pp_part = forward_pp - backward_pp
    cross_full = lax.all_gather(magnus_cross, "row", axis=1, tiled=True)
    backward_cc = contract(hamilton_cross * scale_cc, cross_full)
    forward_cc = fold_rows(
        magnus_cross * scale_cc, lax.all_gather(hamilton_cross, "row", axis=1, tiled=True)
    )
    cross_part = forward_cc - backward_cc
    slot_total = send_order.shape[0] * send_order.shape[1]
    tile_ids = jnp.arange(tile_total, dtype=jnp.int32)
    inverse_recv = jnp.full((slot_total,), tile_total, jnp.int32).at[recv_order].set(tile_ids)
    weighted_cross = jnp.concatenate(
        [(weights * cut_tiles(cross_part)).astype(jnp.bfloat16), blank_tile]
    )
    outgoing_cross = weighted_cross[inverse_recv].reshape(
        send_order.shape[0], send_order.shape[1], TR, COLT
    )
    came_back = lax.all_to_all(outgoing_cross, "chan", split_axis=0, concat_axis=0, tiled=True)
    inverse_send = (
        jnp.zeros((tile_total,), jnp.int32)
        .at[send_order.reshape(-1)]
        .set(jnp.arange(slot_total, dtype=jnp.int32), mode="drop")
    )
    ph_part = join_tiles(
        came_back.reshape(-1, TR, COLT)[inverse_send], slot_count, strip_rows, strip_width
    )
    combined = hamilton_live.astype(jnp.float32) + pp_part + ph_part.astype(jnp.float32)
    flowed = jnp.where(live_mask, combined, jnp.zeros((), jnp.float32)).astype(jnp.bfloat16)
    return (magnus_new, flowed)


def solution(mesh):
    return jax.shard_map(
        per_device,
        mesh=mesh,
        in_specs=(
            P("chan", "row", None),
            P("chan", "row", None),
            P("chan", "row", None),
            P("chan"),
            P(),
            P(),
            P("chan", None),
            P("chan", None, None),
            P("chan", None),
            P("chan", None),
        ),
        out_specs=(P("chan", "row", None), P("chan", "row", None)),
        check_vma=False,
    )
```

profile of v0, /device:TPU:0, one launch (start us, length us, event | category | flops | bytes accessed | tf_op | source)
XLA Modules:
  0.0 224.2 jit_solution(1113929758453855924)
XLA Ops:
  7.9 1.3 fusion.30
  9.2 0.7 iota_compare_fusion
  9.8 0.7 add_compare_fusion
  10.5 5.5 %and_select_fusion.1 = (bf16[1,640,1280]{2,1,0:T(8,128)(2,1)S(1)}, bf16[1,640,1280]{2,1,0:T(8,128)(2,1)}, bf16[1,640,1280]{2,1,0:T(8,128)(2,1)}) fusion(pred[1280]{0:T(1024)(128)(4,1)S(1)} %iota_compare_fusion, pred[640]{0:T(1024)(128)(4,1)S(1)} %add_compare_fusion, bf16[1,640,1280]{2,1,0:T(8,128)(2,1)} %param.10, bf16[1,640,1280]{2,1,0:T(8,128)(2,1)} %param.11, ...), kind=kLoop, calls=%fused_computation.9 | loop fusion | flops 6553600 | bytes 9832320 | tf_op jit(solution)/shard_map/jit(_where)/select_n | solution.py:58
  16.0 2.7 %reshape.337 = bf16[1,16,40,10,128]{4,3,2,1,0:T(8,128)(2,1)} reshape(bf16[1,640,1280]{2,1,0:T(8,128)(2,1)S(1)} %get-tuple-element.6) | data formatting | bytes 3276800 | tf_op jit(solution)/shard_map/reshape | solution.py:15
  18.7 3.4 %copy.18 = bf16[1,16,10,40,128]{4,3,2,1,0:T(8,128)(2,1)} copy(bf16[1,16,10,40,128]{4,2,3,1,0:T(8,128)(2,1)} %bitcast.87) | data formatting | bytes 3276800 | tf_op jit(solution)/shard_map/transpose | solution.py:16
  22.3 1.7 concatenate.9
  24.0 2.3 %gather_fusion = bf16[192,40,128]{2,1,0:T(8,128)(2,1)} fusion(bf16[161,40,128]{2,1,0:T(8,128)(2,1)S(1)} %concatenate.9, s32[1024]{0:T(1024)S(1)} %pad_clamp_fusion.3), kind=kCustom, calls=%fused_computation | custom fusion | bytes 3932928 | tf_op jit(solution)/shard_map/gather | solution.py:65
  26.4 11.9 %all-to-all-start = ((bf16[64,3,40,128]{3,2,1,0:T(8,128)(2,1)}), bf16[64,3,40,128]{3,2,1,0:T(8,128)(2,1)}, u32[]{:S(2)}, u32[]{:S(2)}) async-start(bf16[64,3,40,128]{3,2,1,0:T(8,128)(2,1)} %bitcast.91), calls=%async_computation | async-start | bytes 3932160 | tf_op jit(solution)/shard_map/all_to_all | solution.py:68
  38.2 2.5 %reshape.340 = bf16[1,16,40,10,128]{4,3,2,1,0:T(8,128)(2,1)} reshape(bf16[1,640,1280]{2,1,0:T(8,128)(2,1)S(1)} %copy-done.3) | data formatting | bytes 3276800 | tf_op jit(solution)/shard_map/reshape | solution.py:15
  40.7 2.2 copy.21
  42.9 0.3 concatenate.10
  43.2 2.3 %gather_fusion.2 = bf16[192,40,128]{2,1,0:T(8,128)(2,1)} fusion(bf16[161,40,128]{2,1,0:T(8,128)(2,1)S(1)} %concatenate.10, s32[1024]{0:T(1024)S(1)} %pad_clamp_fusion.3), kind=kCustom, calls=%fused_computation.2 | custom fusion | bytes 3932928 | tf_op jit(solution)/shard_map/gather | solution.py:66
  45.5 21.2 %all-to-all-done = bf16[64,3,40,128]{3,2,1,0:T(8,128)(2,1)} async-done(((bf16[64,3,40,128]{3,2,1,0:T(8,128)(2,1)}), bf16[64,3,40,128]{3,2,1,0:T(8,128)(2,1)}, u32[]{:S(2)}, u32[]{:S(2)}) %all-to-all-start) | async-done | bytes 1966112 | tf_op jit(solution)/shard_map/all_to_all | solution.py:68
  66.7 5.8 %all-to-all-start.1 = ((bf16[64,3,40,128]{3,2,1,0:T(8,128)(2,1)}), bf16[64,3,40,128]{3,2,1,0:T(8,128)(2,1)S(1)}, u32[]{:S(2)}, u32[]{:S(2)}) async-start(bf16[64,3,40,128]{3,2,1,0:T(8,128)(2,1)} %bitcast.90), calls=%async_computation.1 | async-start | bytes 3932160 | tf_op jit(solution)/shard_map/all_to_all | solution.py:69
  72.5 0.6 broadcast.224
  73.1 0.7 reduce.9
  74.0 3.7 %gather_fusion.1 = bf16[160,40,128]{2,1,0:T(8,128)(2,1)} fusion(bf16[192,40,128]{2,1,0:T(8,128)(2,1)} %bitcast.12, s32[1024]{0:T(1024)S(1)} %pad_clamp_fusion.2), kind=kCustom, calls=%fused_computation.1 | custom fusion | bytes 3277440 | tf_op jit(solution)/shard_map/gather | solution.py:73
  77.7 23.2 %all-to-all-done.1 = bf16[64,3,40,128]{3,2,1,0:T(8,128)(2,1)S(1)} async-done(((bf16[64,3,40,128]{3,2,1,0:T(8,128)(2,1)}), bf16[64,3,40,128]{3,2,1,0:T(8,128)(2,1)S(1)}, u32[]{:S(2)}, u32[]{:S(2)}) %all-to-all-start.1) | async-done | bytes 1966112 | tf_op jit(solution)/shard_map/all_to_all | solution.py:69
  100.9 2.2 gather_fusion.3
  103.1 5.3 %broadcast_multiply_fusion.1 = (bf16[1,16,40,10,128]{4,2,3,1,0:T(8,128)(2,1)}, bf16[1,16,40,10,128]{4,2,3,1,0:T(8,128)(2,1)}, bf16[1,16,40,10,128]{4,2,3,1,0:T(8,128)(2,1)}, bf16[1,16,40,10,128]{4,2,3,1,0:T(8,128)(2,1)S(1)}) fusion(bf16[10,128]{1,0:T(8,128)(2,1)S(1)} %bitcast.100, bf16[1,16,10,40,128]{4,3,2,1,0:T(8,128)(2,1)} %bitcast.96, ...), kind=kLoop, calls=%fused_computation.43 | loop fusion | flops 6553600 | bytes 9833600 | tf_op jit(solution)/shard_map/mul | solution.py:94
  108.4 0.6 copy.22
  109.0 2.3 %reshape.343 = bf16[1,640,1280]{2,1,0:T(8,128)(2,1)} reshape(bf16[1,16,40,10,128]{4,3,2,1,0:T(8,128)(2,1)S(1)} %copy.22) | data formatting | bytes 3276800 | tf_op jit(solution)/shard_map/reshape | solution.py:21
  111.4 2.0 copy.24
  113.4 2.3 %reshape.345 = bf16[1,640,1280]{2,1,0:T(8,128)(2,1)} reshape(bf16[1,16,40,10,128]{4,3,2,1,0:T(8,128)(2,1)S(1)} %copy.24) | data formatting | bytes 3276800 | tf_op jit(solution)/shard_map/reshape | solution.py:21
  115.8 0.7 all-gather.5.cloned.1.call-update
  116.6 0.5 all-gather.7.cloned.1.call-update
  117.1 1.3 scatter_custom_fusion
  118.4 2.0 copy.20
  120.5 0.6 copy.23
  121.1 2.0 all-gather.9.cloned.1.call-done
  123.1 6.7 %fusion.7 = f32[640,1280]{1,0:T(8,128)} fusion(bf16[1,1280,1280]{2,1,0:T(8,128)(2,1)} %all-gather.9.cloned.1.call-done, bf16[80,8,10,128]{3,2,1,0:T(8,128)(2,1)} %bitcast.99), kind=kOutput, calls=%fused_computation.24 | convolution fusion | flops 2097152000 | bytes 8192000 | tf_op jit(solution)/shard_map/sik,skj->sij/dot_general | solution.py:25
  129.8 11.3 %all-gather.11.cloned.1.call-done = bf16[1,1280,1280]{2,1,0:T(8,128)(2,1)} async-done(((bf16[1,640,1280]{2,1,0:T(8,128)(2,1)}), bf16[1,1280,1280]{2,1,0:T(8,128)(2,1)}) %all-gather.11.cloned.1.call-update) | async-done | bytes 3276816 | tf_op jit(solution)/shard_map/all_gather | solution.py:91
  141.1 6.9 %convolution_subtract_fusion = f32[640,1280]{1,0:T(8,128)} fusion(f32[640,1280]{1,0:T(8,128)} %fusion.7, bf16[1,1280,1280]{2,1,0:T(8,128)(2,1)} %all-gather.11.cloned.1.call-done, bf16[80,8,10,128]{3,2,1,0:T(8,128)(2,1)S(1)} %bitcast.98), kind=kOutput, calls=%fused_computation.11 | convolution fusion | flops 2097971200 | bytes 11468800 | tf_op jit(solution)/shard_map/sik,skj->sij/dot_general | solution.py:25
  148.1 4.9 %reshape.347 = f32[1,16,40,10,128]{4,3,2,1,0:T(8,128)} reshape(f32[640,1280]{1,0:T(8,128)} %convolution_subtract_fusion) | data formatting | bytes 6553600 | tf_op jit(solution)/shard_map/reshape | solution.py:15
  152.9 4.2 %copy.25 = f32[1,16,10,40,128]{4,3,2,1,0:T(8,128)S(1)} copy(f32[1,16,10,40,128]{4,2,3,1,0:T(8,128)} %bitcast.86) | data formatting | bytes 6553600 | tf_op jit(solution)/shard_map/transpose | solution.py:16
  157.1 0.3 fusion.5
  157.5 0.3 concatenate.11
  157.7 2.2 %gather_fusion.4 = bf16[192,40,128]{2,1,0:T(8,128)(2,1)} fusion(bf16[161,40,128]{2,1,0:T(8,128)(2,1)S(1)} %concatenate.11, s32[1024]{0:T(1024)S(1)} %pad_clamp_fusion.1), kind=kCustom, calls=%fused_computation.4 | custom fusion | bytes 3932928 | tf_op jit(solution)/shard_map/gather | solution.py:103
  160.0 10.8 %all-to-all-start.2 = ((bf16[64,3,40,128]{3,2,1,0:T(8,128)(2,1)}), bf16[64,3,40,128]{3,2,1,0:T(8,128)(2,1)}, u32[]{:S(2)}, u32[]{:S(2)}) async-start(bf16[64,3,40,128]{3,2,1,0:T(8,128)(2,1)} %bitcast.89), calls=%async_computation.2 | async-start | bytes 3932160 | tf_op jit(solution)/shard_map/all_to_all | solution.py:106
  171.0 1.4 scatter_custom_fusion.1
  172.5 0.2 convolution_reduce_fusion
  172.8 6.4 %fusion.10 = f32[640,1280]{1,0:T(8,128)} fusion(bf16[1,1280,1280]{2,1,0:T(8,128)(2,1)} %all-gather.5.cloned.1.call-done, bf16[1,640,1280]{2,1,0:T(8,128)(2,1)S(1)} %copy-done.2, bf16[1280]{0:T(1024)(128)(2,1)S(1)} %convolution_reduce_fusion), kind=kOutput, calls=%fused_computation.27 | convolution fusion | flops 2097971200 | bytes 8194560 | tf_op jit(solution)/shard_map/sik,skj->sij/dot_general | solution.py:25
  179.1 20.7 %all-to-all-done.2 = bf16[64,3,40,128]{3,2,1,0:T(8,128)(2,1)} async-done(((bf16[64,3,40,128]{3,2,1,0:T(8,128)(2,1)}), bf16[64,3,40,128]{3,2,1,0:T(8,128)(2,1)}, u32[]{:S(2)}, u32[]{:S(2)}) %all-to-all-start.2) | async-done | bytes 1966112 | tf_op jit(solution)/shard_map/all_to_all | solution.py:106
  199.8 2.5 %gather_fusion.5 = bf16[160,40,128]{2,1,0:T(8,128)(2,1)S(1)} fusion(bf16[192,40,128]{2,1,0:T(8,128)(2,1)} %bitcast.28, s32[1024]{0:T(1024)S(1)} %pad_clamp_fusion), kind=kCustom, calls=%fused_computation.5 | custom fusion | bytes 3277440 | tf_op jit(solution)/shard_map/gather | solution.py:113
  202.6 3.1 %copy.27 = f32[1,16,40,10,128]{4,3,2,1,0:T(8,128)} copy(f32[1,16,40,10,128]{4,2,3,1,0:T(8,128)S(1)} %convert_bitcast_fusion) | data formatting | bytes 6553600 | tf_op jit(solution)/shard_map/convert_element_type | solution.py:115
  205.7 5.0 %reshape.353 = f32[1,640,1280]{2,1,0:T(8,128)} reshape(f32[1,16,40,10,128]{4,3,2,1,0:T(8,128)} %copy.27) | data formatting | bytes 6553600 | tf_op jit(solution)/shard_map/convert_element_type | solution.py:115
  210.7 7.0 %fusion.12 = bf16[1,640,1280]{2,1,0:T(8,128)(2,1)} fusion(f32[1,640,1280]{2,1,0:T(8,128)} %reshape.353, f32[640,1280]{1,0:T(8,128)} %fusion.10, bf16[1,1280,1280]{2,1,0:T(8,128)(2,1)} %all-gather.7.cloned.1.call-done, pred[1280]{0:T(1024)(128)(4,1)S(1)} %iota_compare_fusion, pred[640]{0:T(1024)(128)(4,1)S(1)} %add_compare_fusion, ...), kind=kOutput, calls=%fused_computation.30 | convolution fusion | flops 2108620800 | bytes 13111680 | tf_op jit(solution)/shard_map/sik,skj->sij/dot_general | solution.py:25
  (48 shorter events, 1.1 us)
Async XLA Ops:
  7.2 165.3 %copy-start = (f32[64,1280]{1,0:T(8,128)S(1)}, f32[64,1280]{1,0:T(8,128)}, u32[]{:S(2)}) copy-start(f32[64,1280]{1,0:T(8,128)} %param.15) | copy-start | bytes 983044
  16.0 2.7 %copy-start.1 = (bf16[1,640,1280]{2,1,0:T(8,128)(2,1)}, bf16[1,640,1280]{2,1,0:T(8,128)(2,1)S(1)}, u32[]{:S(2)}) copy-start(bf16[1,640,1280]{2,1,0:T(8,128)(2,1)S(1)} %get-tuple-element.6) | copy-start | bytes 4915204
  18.7 3.4 %copy-start.7 = (s32[1,64,3]{1,0,2:T(1,128)S(1)}, s32[1,64,3]{1,0,2:T(1,128)}, u32[]{:S(2)}) copy-start(s32[1,64,3]{1,0,2:T(1,128)} %param.17) | copy-start | bytes 2308
  26.4 11.9 %copy-start.3 = (bf16[1,640,1280]{2,1,0:T(8,128)(2,1)S(1)}, bf16[1,640,1280]{2,1,0:T(8,128)(2,1)}, u32[]{:S(2)}) copy-start(bf16[1,640,1280]{2,1,0:T(8,128)(2,1)} %get-tuple-element.10) | copy-start | bytes 4915204
  26.4 40.3 %all-to-all-start = ((bf16[64,3,40,128]{3,2,1,0:T(8,128)(2,1)}), bf16[64,3,40,128]{3,2,1,0:T(8,128)(2,1)}, u32[]{:S(2)}, u32[]{:S(2)}) async-start(bf16[64,3,40,128]{3,2,1,0:T(8,128)(2,1)} %bitcast.91), calls=%async_computation | async-start | bytes 3932160 | tf_op jit(solution)/shard_map/all_to_all | solution.py:68
  66.7 6.4 %copy-start.9 = (f32[1,160]{1,0:T(1,128)S(1)}, f32[1,160]{1,0:T(1,128)}, u32[]{:S(2)}) copy-start(f32[1,160]{1,0:T(1,128)} %param.19) | copy-start | bytes 1924
  66.7 7.2 %copy-start.10 = (s32[1,160]{1,0:T(1,128)S(1)}, s32[1,160]{1,0:T(1,128)}, u32[]{:S(2)}) copy-start(s32[1,160]{1,0:T(1,128)} %param.18) | copy-start | bytes 1924
  66.7 7.3 %copy-start.8 = (f32[1,1280]{1,0:T(1,128)S(1)}, f32[1,1280]{1,0:T(1,128)}, u32[]{:S(2)}) copy-start(f32[1,1280]{1,0:T(1,128)} %param.16) | copy-start | bytes 15364
  66.7 34.3 %all-to-all-start.1 = ((bf16[64,3,40,128]{3,2,1,0:T(8,128)(2,1)}), bf16[64,3,40,128]{3,2,1,0:T(8,128)(2,1)S(1)}, u32[]{:S(2)}, u32[]{:S(2)}) async-start(bf16[64,3,40,128]{3,2,1,0:T(8,128)(2,1)} %bitcast.90), calls=%async_computation.1 | async-start | bytes 3932160 | tf_op jit(solution)/shard_map/all_to_all | solution.py:69
  72.5 50.6 %all-gather.9.cloned.1.call-start = ((), (), s32[]{:S(2)}) async-start(), calls=%async_computation.5 | async-start | bytes 4915200 | tf_op jit(solution)/shard_map/all_gather | solution.py:94
  111.4 29.8 %all-gather.11.cloned.1.call-start = ((), (), s32[]{:S(2)}) async-start(), calls=%async_computation.6 | async-start | bytes 4915200 | tf_op jit(solution)/shard_map/all_gather | solution.py:91
  115.8 2.6 %copy-start.5 = (bf16[1,16,40,10,128]{4,2,3,1,0:T(8,128)(2,1)S(1)}, bf16[1,16,40,10,128]{4,2,3,1,0:T(8,128)(2,1)}, u32[]{:S(2)}) copy-start(bf16[1,16,40,10,128]{4,2,3,1,0:T(8,128)(2,1)} %get-tuple-element.4) | copy-start | bytes 4915204
  115.8 57.0 %all-gather.5.cloned.1.call-start = ((), (), s32[]{:S(2)}) async-start(), calls=%async_computation.3 | async-start | bytes 4915200 | tf_op jit(solution)/shard_map/all_gather | solution.py:86
  116.5 94.2 %all-gather.7.cloned.1.call-start = ((), (), s32[]{:S(2)}) async-start(), calls=%async_computation.4 | async-start | bytes 4915200 | tf_op jit(solution)/shard_map/all_gather | solution.py:88
  118.4 2.0 copy-start.4
  160.0 12.8 %copy-start.2 = (bf16[1,640,1280]{2,1,0:T(8,128)(2,1)S(1)}, bf16[1,640,1280]{2,1,0:T(8,128)(2,1)}, u32[]{:S(2)}) copy-start(bf16[1,640,1280]{2,1,0:T(8,128)(2,1)} %copy-done.1) | copy-start | bytes 4915204
  160.0 39.8 %all-to-all-start.2 = ((bf16[64,3,40,128]{3,2,1,0:T(8,128)(2,1)}), bf16[64,3,40,128]{3,2,1,0:T(8,128)(2,1)}, u32[]{:S(2)}, u32[]{:S(2)}) async-start(bf16[64,3,40,128]{3,2,1,0:T(8,128)(2,1)} %bitcast.89), calls=%async_computation.2 | async-start | bytes 3932160 | tf_op jit(solution)/shard_map/all_to_all | solution.py:106
  205.7 5.0 %copy-start.6 = (bf16[1,640,1280]{2,1,0:T(8,128)(2,1)S(1)}, bf16[1,640,1280]{2,1,0:T(8,128)(2,1)}, u32[]{:S(2)}) copy-start(bf16[1,640,1280]{2,1,0:T(8,128)(2,1)} %param.12) | copy-start | bytes 4915204
Sparse Core Ops, SparseCore 0:
  111.5 11.5 all-gather.8
  124.8 16.3 all-gather.10
  143.4 16.3 all-gather.4
  161.3 16.3 all-gather.6
where the time goes:
time: 225 us; the launch traced here: 224 us
  waiting for transfers between devices  79.7 us (35%)
  local copies, waits for them, and re-layouts  59.2 us (26%)
  starting transfers between devices  28.6 us (13%)
  matrix products  27.2 us (12%)
  between operations  14.8 us (7%)
  other arithmetic  14.7 us (7%)
    dot_general x4, matrix products, contract(): jnp.einsum('sik,skj->sij', left_side, right_side, preferred_element_type=...  27 us
    all_to_all x1, waiting for transfers between devices, per_device(): lax.all_to_all(outgoing_hamilton, 'chan', split_axis=0, concat_axis=0, ti...  23.2 us
    all_to_all x1, waiting for transfers between devices, per_device(): lax.all_to_all(outgoing_magnus, 'chan', split_axis=0, concat_axis=0, tile...  21.2 us
    all_to_all x1, waiting for transfers between devices, per_device(): lax.all_to_all(outgoing_cross, 'chan', split_axis=0, concat_axis=0, tiled...  20.7 us
    all_to_all x1, starting transfers between devices, per_device(): lax.all_to_all(outgoing_magnus, 'chan', split_axis=0, concat_axis=0, tile...  11.9 us
    all_gather x1, waiting for transfers between devices, per_device(): cross_full = lax.all_gather(magnus_cross, 'row', axis=1, tiled=True)  11.3 us
    all_to_all x1, starting transfers between devices, per_device(): lax.all_to_all(outgoing_cross, 'chan', split_axis=0, concat_axis=0, tiled...  10.8 us
    reshape x3, local copies, waits for them, and re-layouts, cut_tiles(): strip.reshape(slot_count, strip_rows // TR, TR, strip_width // COLT, COLT)  10.1 us
  transfers between devices with their start and end apart: 7, of which 5 were waited for; matrix products, arithmetic and copies ran while one was open for 29% of the time, Pallas kernels for 0%

commit v1 on v0

v1 whole, which is shorter than its diff:
```python
import functools

import jax
import jax.numpy as jnp
from jax import lax
from jax.experimental import pallas as pl
from jax.experimental.pallas import tpu as pltpu
from jax.sharding import PartitionSpec as P

TR = 40
COLT = 128
SLOTS = 3
STEP_SIZE = 0.5
PEERS = 64
MULT = 37
MESH = pl.DeviceIdType.MESH
F32 = jnp.float32
BF16 = jnp.bfloat16

ROWS = 640
WIDTH = 1280
BLOCKS = WIDTH // COLT
PAIRS = ROWS // (2 * TR)
TILES = (ROWS // TR) * BLOCKS
PAIR = 2 * TR
BACK = 128
CHUNK = 256


def spin(me, step, sign):
    off = lax.rem(step * MULT, PEERS)
    x = lax.rem(lax.rem(me, 4) + 4 + sign * lax.rem(off, 4), 4)
    y = lax.rem(lax.rem(lax.div(me, 4), 4) + 4 + sign * lax.rem(lax.div(off, 4), 4), 4)
    z = lax.rem(lax.div(me, 16) + 4 + sign * lax.div(off, 16), 4)
    return (z * 4 + y) * 4 + x


def rows_at(start, size, unit):
    return pl.ds(pl.multiple_of(start, unit), size)


def kernel(
    gen, mag, ham, slot_ref, dims_ref, pp_ref, cc_ref, send_ref, recv_ref, weight_ref,
    new_out, flow_out,
    gen_v, mag_v, ham_v, pp_v, stack, sbuf, near, far, right, left, base, cross, tsend, trecv, unpacked,
    inv_v, inv_s,
    in_sem, pp_sem, inv_sem, out_sem, new_sem, self_sem, send_sem, recv_sem, hand_sem, take_sem,
    strip_send, strip_recv, bsend_sem, brecv_sem, bself_sem,
):
    me = lax.axis_index("chan")
    row = lax.axis_index("row")
    other = 1 - row

    def load(i, start):
        for n, (src, dst) in enumerate(((gen, gen_v), (mag, mag_v), (ham, ham_v))):
            at = rows_at(i * PAIR, PAIR, 16)
            copy = pltpu.make_async_copy(src.at[0, at], dst.at[at], in_sem.at[n, i])
            copy.start() if start else copy.wait()

    for i in range(PAIRS):
        load(i, True)
    pp_copy = pltpu.make_async_copy(pp_ref, pp_v, pp_sem)
    pp_copy.start()
    barrier = pltpu.get_barrier_semaphore()

    def greet(step, _):
        pl.semaphore_signal(
            barrier, inc=1, device_id={"chan": spin(me, step, 1)}, device_id_type=MESH
        )
        return 0

    lax.fori_loop(1, PEERS, greet, 0)
    pl.semaphore_signal(barrier, inc=1, device_id={"row": other}, device_id_type=MESH)

    limit = dims_ref[slot_ref[0]]

    def live(i, k):
        row_ids = row * ROWS + i * PAIR + lax.broadcasted_iota(jnp.int32, (PAIR, COLT), 0)
        col_ids = k * COLT + lax.broadcasted_iota(jnp.int32, (PAIR, COLT), 1)
        return (row_ids < limit) & (col_ids < limit)

    def prologue(i, _):
        load(i, False)
        at = rows_at(i * PAIR, PAIR, 16)
        for k in range(BLOCKS):
            col = pl.ds(k * COLT, COLT)
            new = (mag_v[at, col].astype(F32) + STEP_SIZE * gen_v[at, col].astype(F32)).astype(BF16)
            mag_v[at, col] = new
            mask = live(i, k)
            m = jnp.where(mask, new.astype(F32), 0.0)
            h = jnp.where(mask, ham_v[at, col].astype(F32), 0.0)
            for half in range(2):
                cut = slice(half * TR, (half + 1) * TR)
                tile = (2 * i + half) * BLOCKS + k
                stack[tile] = jnp.concatenate([m[cut], h[cut]], axis=0).astype(BF16)
        return 0

    lax.fori_loop(0, PAIRS, prologue, 0)
    new_copy = pltpu.make_async_copy(mag_v, new_out.at[0], new_sem)
    new_copy.start()
    pl.semaphore_wait(barrier, PEERS)

    def pick(to):
        for l in range(SLOTS):
            tile = jnp.minimum(send_ref[0, to, l], TILES - 1)
            sbuf[to * SLOTS + l] = stack[tile]

    def message(step):
        to = spin(me, step, 1)
        return pltpu.make_async_remote_copy(
            sbuf.at[pl.ds(to * SLOTS, SLOTS)],
            near.at[pl.ds(me * SLOTS, SLOTS)],
            send_sem.at[step],
            recv_sem.at[step],
            device_id={"chan": to},
            device_id_type=MESH,
        )

    def arrival(step):
        fr = spin(me, step, -1)
        return pltpu.make_async_remote_copy(
            sbuf.at[pl.ds(fr * SLOTS, SLOTS)],
            near.at[pl.ds(fr * SLOTS, SLOTS)],
            send_sem.at[step],
            recv_sem.at[step],
            device_id={"chan": fr},
            device_id_type=MESH,
        )

    def handed(step):
        at = pl.ds(spin(me, step, -1) * SLOTS, SLOTS)
        return pltpu.make_async_remote_copy(
            near.at[at], far.at[at], hand_sem.at[step], take_sem.at[step],
            device_id={"row": other}, device_id_type=MESH,
        )

    def send_out(step, _):
        pick(spin(me, step, 1))
        message(step).start()
        return 0

    lax.fori_loop(1, PEERS, send_out, 0)
    pick(me)
    mine = pltpu.make_async_copy(
        sbuf.at[pl.ds(me * SLOTS, SLOTS)], near.at[pl.ds(me * SLOTS, SLOTS)], self_sem
    )
    mine.start()

    pp_copy.wait()
    chosen = lax.broadcasted_iota(jnp.int32, pp_v.shape, 0) == slot_ref[0]
    factor = jnp.sum(jnp.where(chosen, pp_v[...], 0.0), axis=0, keepdims=True)

    def strips(i, _):
        at = rows_at(i * PAIR, PAIR, 16)
        for k in range(BLOCKS):
            col = pl.ds(k * COLT, COLT)
            mask = live(i, k)
            m = jnp.where(mask, mag_v[at, col].astype(F32), 0.0)
            h = jnp.where(mask, ham_v[at, col].astype(F32), 0.0)
            f = factor[:, k * COLT : (k + 1) * COLT]
            right[rows_at(row * ROWS + i * PAIR, PAIR, 16), col] = h.astype(BF16)
            right[rows_at(WIDTH + row * ROWS + i * PAIR, PAIR, 16), col] = m.astype(BF16)
            left[at, col] = (m * f).astype(BF16)
            left[at, pl.ds(WIDTH + k * COLT, COLT)] = (h * -f).astype(BF16)
            base[rows_at(k * ROWS + i * PAIR, PAIR, 8), :] = h
        return 0

    lax.fori_loop(0, PAIRS, strips, 0)

    def strip(which, r):
        at = rows_at(which * WIDTH + r * ROWS, ROWS, 16)
        return pltpu.make_async_remote_copy(
            right.at[at], right.at[at], strip_send.at[which], strip_recv.at[which],
            device_id={"row": other}, device_id_type=MESH,
        )

    for which in range(2):
        strip(which, row).start()
    mine.wait()
    handed(0).start()

    place = lax.broadcasted_iota(jnp.int32, (8, COLT), 0) * COLT + lax.broadcasted_iota(
        jnp.int32, (8, COLT), 1
    )

    def invert_recv(v, table):
        return jnp.where(place == recv_ref[0, v], v, table)

    def invert_send(d, table):
        for l in range(SLOTS):
            table = jnp.where(place == send_ref[0, d, l], d * SLOTS + l, table)
        return table

    blank = jnp.zeros((8, COLT), jnp.int32)
    inv_v[0] = lax.fori_loop(0, TILES, invert_recv, blank)
    inv_v[1] = lax.fori_loop(0, PEERS, invert_send, blank)
    inv_copy = pltpu.make_async_copy(inv_v, inv_s, inv_sem)
    inv_copy.start()

    for which in range(2):
        strip(which, other).wait_recv()
        strip(which, row).wait_send()

    def pp_product(n, _):
        col = pl.ds(pl.multiple_of(n * CHUNK, CHUNK), CHUNK)
        part = jnp.dot(left[...], right[:, col], preferred_element_type=F32)
        for half in range(CHUNK // COLT):
            at = rows_at((n * (CHUNK // COLT) + half) * ROWS, ROWS, 8)
            base[at, :] += part[:, half * COLT : (half + 1) * COLT]
        return 0

    lax.fori_loop(0, WIDTH // CHUNK, pp_product, 0)
    inv_copy.wait()

    def hand_on(step, _):
        arrival(step).wait_recv()
        handed(step).start()
        return 0

    lax.fori_loop(1, PEERS, hand_on, 0)

    def settle(tiles, r, own):
        def body(i, _):
            at = rows_at(r * ROWS + i * PAIR, PAIR, 16)
            under = rows_at(WIDTH + r * ROWS + i * PAIR, PAIR, 16)
            for k in range(BLOCKS):
                col = pl.ds(k * COLT, COLT)
                parts = []
                for half in range(2):
                    v = (2 * i + half) * BLOCKS + k
                    tile = tiles[recv_ref[0, v]]
                    parts.append(weight_ref[0, v] * tile.astype(F32))
                m = jnp.concatenate([parts[0][:TR], parts[1][:TR]], axis=0)
                h = jnp.concatenate([parts[0][TR:], parts[1][TR:]], axis=0)
                right[at, col] = h.astype(BF16)
                right[under, col] = m.astype(BF16)
                if own:
                    f = cc_ref[:, k * COLT : (k + 1) * COLT]
                    here = rows_at(i * PAIR, PAIR, 16)
                    left[here, col] = (m * f).astype(BF16)
                    left[here, pl.ds(WIDTH + k * COLT, COLT)] = (h * -f).astype(BF16)
            return 0

        lax.fori_loop(0, PAIRS, body, 0)

    settle(near, row, True)

    def take(step, _):
        handed(step).wait_recv()
        return 0

    lax.fori_loop(0, PEERS, take, 0)
    settle(far, other, False)

    def cc_product(n, _):
        col = pl.ds(pl.multiple_of(n * CHUNK, CHUNK), CHUNK)
        part = jnp.dot(left[...], right[:, col], preferred_element_type=F32)
        for half in range(CHUNK // COLT):
            for a in range(ROWS // TR):
                tile = a * BLOCKS + n * (CHUNK // COLT) + half
                cross[tile] = part[a * TR : (a + 1) * TR, half * COLT : (half + 1) * COLT]
        return 0

    lax.fori_loop(0, WIDTH // CHUNK, cc_product, 0)

    def pick_back(to):
        parts = []
        for l in range(SLOTS):
            slot = to * SLOTS + l
            v = inv_s[0, lax.div(slot, COLT), lax.rem(slot, COLT)]
            parts.append(weight_ref[0, v] * cross[v])
        parts.append(jnp.zeros((BACK - SLOTS * TR, COLT), F32))
        tsend[rows_at(to * BACK, BACK, 16), :] = jnp.concatenate(parts, axis=0).astype(BF16)

    def back(step):
        to = spin(me, step, 1)
        return pltpu.make_async_remote_copy(
            tsend.at[rows_at(to * BACK, BACK, 16)],
            trecv.at[rows_at(me * BACK, BACK, 16)],
            bsend_sem.at[step],
            brecv_sem.at[step],
            device_id={"chan": to},
            device_id_type=MESH,
        )

    def back_arrival(step):
        fr = spin(me, step, -1)
        return pltpu.make_async_remote_copy(
            tsend.at[rows_at(fr * BACK, BACK, 16)],
            trecv.at[rows_at(fr * BACK, BACK, 16)],
            bsend_sem.at[step],
            brecv_sem.at[step],
            device_id={"chan": fr},
            device_id_type=MESH,
        )

    def send_back(step, _):
        pick_back(spin(me, step, 1))
        back(step).start()
        return 0

    lax.fori_loop(1, PEERS, send_back, 0)
    pick_back(me)
    home = pltpu.make_async_copy(
        tsend.at[rows_at(me * BACK, BACK, 16)], trecv.at[rows_at(me * BACK, BACK, 16)], bself_sem
    )
    home.start()

    def unpack(fr):
        rows = trecv[rows_at(fr * BACK, BACK, 16), :].astype(F32)
        for l in range(SLOTS):
            unpacked[fr * SLOTS + l] = rows[l * TR : (l + 1) * TR]

    home.wait()
    unpack(me)

    def take_back(step, _):
        back_arrival(step).wait_recv()
        unpack(spin(me, step, -1))
        return 0

    lax.fori_loop(1, PEERS, take_back, 0)

    def out_copy(i):
        at = rows_at(i * PAIR, PAIR, 16)
        return pltpu.make_async_copy(gen_v.at[at], flow_out.at[0, at], out_sem.at[i])

    def finish(i, _):
        at = rows_at(i * PAIR, PAIR, 16)
        for k in range(BLOCKS):
            parts = []
            for half in range(2):
                u = (2 * i + half) * BLOCKS + k
                slot = inv_s[1, lax.div(u, COLT), lax.rem(u, COLT)]
                parts.append(unpacked[slot])
            total = base[rows_at(k * ROWS + i * PAIR, PAIR, 8), :] + jnp.concatenate(parts, axis=0)
            gen_v[at, pl.ds(k * COLT, COLT)] = jnp.where(live(i, k), total, 0.0).astype(BF16)
        out_copy(i).start()
        return 0

    lax.fori_loop(0, PAIRS, finish, 0)

    def drain(step, _):
        message(step).wait_send()
        handed(step).wait_send()
        back(step).wait_send()
        return 0

    lax.fori_loop(1, PEERS, drain, 0)
    handed(0).wait_send()
    new_copy.wait()
    for i in range(PAIRS):
        out_copy(i).wait()


def per_device(*args):
    strip = jax.ShapeDtypeStruct(args[0].shape, BF16)
    hbm = pl.BlockSpec(memory_space=pltpu.HBM)
    smem = pl.BlockSpec(memory_space=pltpu.SMEM)
    vmem = pl.BlockSpec(memory_space=pltpu.VMEM)
    dma = pltpu.SemaphoreType.DMA
    return pl.pallas_call(
        kernel,
        out_shape=(strip, strip),
        in_specs=[hbm, hbm, hbm, smem, smem, hbm, vmem, smem, smem, smem],
        out_specs=(hbm, hbm),
        scratch_shapes=[
            pltpu.VMEM((ROWS, WIDTH), BF16),
            pltpu.VMEM((ROWS, WIDTH), BF16),
            pltpu.VMEM((ROWS, WIDTH), BF16),
            pltpu.VMEM((PEERS, WIDTH), F32),
            pltpu.VMEM((TILES, PAIR, COLT), BF16),
            pltpu.VMEM((PEERS * SLOTS, PAIR, COLT), BF16),
            pltpu.VMEM((PEERS * SLOTS, PAIR, COLT), BF16),
            pltpu.VMEM((PEERS * SLOTS, PAIR, COLT), BF16),
            pltpu.VMEM((2 * WIDTH, WIDTH), BF16),
            pltpu.VMEM((ROWS, 2 * WIDTH), BF16),
            pltpu.VMEM((BLOCKS * ROWS, COLT), F32),
            pltpu.VMEM((TILES, TR, COLT), F32),
            pltpu.VMEM((PEERS * BACK, COLT), BF16),
            pltpu.VMEM((PEERS * BACK, COLT), BF16),
            pltpu.VMEM((PEERS * SLOTS, TR, COLT), F32),
            pltpu.VMEM((2, 8, COLT), jnp.int32),
            pltpu.SMEM((2, 8, COLT), jnp.int32),
            dma((3, PAIRS)),
            dma,
            dma,
            dma((PAIRS,)),
            dma,
            dma,
            dma((PEERS,)),
            dma((PEERS,)),
            dma((PEERS,)),
            dma((PEERS,)),
            dma((2,)),
            dma((2,)),
            dma((PEERS,)),
            dma((PEERS,)),
            dma,
        ],
        compiler_params=pltpu.CompilerParams(
            collective_id=0, has_side_effects=True, vmem_limit_bytes=58 << 20
        ),
    )(*args)


def solution(mesh):
    return jax.shard_map(
        per_device,
        mesh=mesh,
        in_specs=(
            P("chan", "row", None),
            P("chan", "row", None),
            P("chan", "row", None),
            P("chan"),
            P(),
            P(),
            P("chan", None),
            P("chan", None, None),
            P("chan", None),
            P("chan", None),
        ),
        out_specs=(P("chan", "row", None), P("chan", "row", None)),
        check_vma=False,
    )
```

time: 225 us -> 106 us (0.47)
  Pallas kernels: 0 us -> 98.8 us
  waiting for transfers between devices: 79.7 us -> 0 us
  local copies, waits for them, and re-layouts: 59.2 us -> 5.37 us
  starting transfers between devices: 28.6 us -> 0 us
  matrix products: 27.2 us -> 0 us
  other arithmetic: 14.7 us -> 0 us
  between operations: 14.8 us -> 1.29 us
    pallas_call x0 -> x1, Pallas kernels: none -> 98.8 us  [per_device(): pl.pallas_call(kernel, out_shape=(strip, strip), in_specs=[hbm, hbm, hbm,...]
    all_to_all x3 -> x0, waiting for transfers between devices: 65.1 us -> none  [the longest x1 23.2 us: per_device(): lax.all_to_all(outgoing_hamilton, 'chan', split_axis=0, concat_axis=0, ti...]
    all_to_all x3 -> x0, starting transfers between devices: 28.4 us -> none  [the longest x1 11.9 us: per_device(): lax.all_to_all(outgoing_magnus, 'chan', split_axis=0, concat_axis=0, tile...]
    dot_general x5 -> x0, matrix products: 27.2 us -> none  [the longest x4 27 us: contract(): jnp.einsum('sik,skj->sij', left_side, right_side, preferred_element_type=...]
    gather x6 -> x0, local copies, waits for them, and re-layouts: 15.3 us -> none  [the longest x2 5.89 us: settle(): picked = arrived.reshape(-1, TR, COLT)[recv_order]]
    reshape x5 -> x0, local copies, waits for them, and re-layouts: 14.7 us -> none  [the longest x3 10.1 us: cut_tiles(): strip.reshape(slot_count, strip_rows // TR, TR, strip_width // COLT, COLT)]
    all_gather x4 -> x0, waiting for transfers between devices: 13.4 us -> none  [the longest x1 11.3 us: per_device(): cross_full = lax.all_gather(magnus_cross, 'row', axis=1, tiled=True)]
    transpose x5 -> x0, local copies, waits for them, and re-layouts: 12.3 us -> none  [the longest x3 9.69 us: cut_tiles(): return tile_grid.transpose(0, 1, 3, 2, 4).reshape(-1, TR, COLT)]
  transfers between devices with their start and end apart: 7 -> 0, of which waited for: 5 -> 0; matrix products, arithmetic and copies ran while one was open for 29% -> 0% of each run, Pallas kernels for 0% -> 0%
where the time goes in v1:
time: 106 us; the launch traced here: 105 us
  Pallas kernels  98.8 us (93%)
  local copies, waits for them, and re-layouts  5.37 us (5%)
  between operations  1.29 us (1%)
    pallas_call x1, Pallas kernels, per_device(): pl.pallas_call(kernel, out_shape=(strip, strip), in_specs=[hbm, hbm, hbm,...  98.8 us
    unnamed x5, local copies, waits for them, and re-layouts  5.37 us

profile of v1, /device:TPU:0, one launch (start us, length us, event | category | flops | bytes accessed | tf_op | source)
XLA Modules:
  0.0 105.5 jit_solution(8740869506151757068)
XLA Ops:
  1.3 1.4 %copy.12.send_ref = s32[1,64,3]{2,1,0:T(8,128)} copy(s32[1,64,3]{1,0,2:T(1,128)} %param.17) | data formatting | bytes 1536 | tf_op args[7]
  2.7 98.8 %shard_map.113 = (bf16[1,640,1280]{2,1,0:T(8,128)(2,1)}, bf16[1,640,1280]{2,1,0:T(8,128)(2,1)}) custom-call(bf16[1,640,1280]{2,1,0:T(8,128)(2,1)} %gen.1, bf16[1,640,1280]{2,1,0:T(8,128)(2,1)} %mag.1, bf16[1,640,1280]{2,1,0:T(8,128)(2,1)} %ham.1, s32[1]{0:T(128)S(6)} %copy.15.slot_ref, s32[64]{0:T(128)} %dims_ref.1, f32[64,1280]{1,0:T(8,128)} %pp_ref.1, ...), custom_call_target="tpu_custom_call" | custom-call | tf_op jit(solution)/shard_map/pallas_call | solution.py:362
  101.5 0.0 copy-start
  101.5 2.8 %copy.16 = bf16[1,640,1280]{2,1,0:T(8,128)(2,1)} copy(bf16[1,640,1280]{2,1,0:T(8,128)(2,1)} %get-tuple-element.4) | data formatting | bytes 3276800
  104.3 0.0 copy-done
  104.3 1.2 %copy.17 = bf16[1,640,1280]{2,1,0:T(8,128)(2,1)} copy(bf16[1,640,1280]{2,1,0:T(8,128)(2,1)S(1)} %copy-done) | data formatting | bytes 3276800
Async XLA Ops:
  101.5 2.8 %copy-start = (bf16[1,640,1280]{2,1,0:T(8,128)(2,1)S(1)}, bf16[1,640,1280]{2,1,0:T(8,128)(2,1)}, u32[]{:S(2)}) copy-start(bf16[1,640,1280]{2,1,0:T(8,128)(2,1)} %get-tuple-element.5) | copy-start | bytes 4915204

commit v2 on v1

--- a/solution.py
+++ b/solution.py
@@ -24,7 +24,6 @@
 TILES = (ROWS // TR) * BLOCKS
 PAIR = 2 * TR
 BACK = 128
-CHUNK = 256
 
 
 def spin(me, step, sign):
@@ -40,11 +39,12 @@
 
 
 def kernel(
-    gen, mag, ham, slot_ref, dims_ref, pp_ref, cc_ref, send_ref, recv_ref, weight_ref,
-    new_out, flow_out,
-    gen_v, mag_v, ham_v, pp_v, stack, sbuf, near, far, right, left, base, cross, tsend, trecv, unpacked,
+    gen, mag, ham, slot_ref, dims_in, pp_in, cc_in, send_in, recv_in, weight_in,
+    flow_out,
+    dims_ref, pp_v, cc_ref, send_ref, recv_ref, weight_ref, small_sem,
+    gen_v, mag_v, ham_v, stack, sbuf, near, far, right, left, base, cross, tsend, trecv, unpacked,
     inv_v, inv_s,
-    in_sem, pp_sem, inv_sem, out_sem, new_sem, self_sem, send_sem, recv_sem, hand_sem, take_sem,
+    in_sem, inv_sem, out_sem, self_sem, send_sem, recv_sem, hand_sem, take_sem,
     strip_send, strip_recv, bsend_sem, brecv_sem, bself_sem,
 ):
     me = lax.axis_index("chan")
@@ -59,8 +59,21 @@
 
     for i in range(PAIRS):
         load(i, True)
-    pp_copy = pltpu.make_async_copy(pp_ref, pp_v, pp_sem)
-    pp_copy.start()
+    small = [
+        pltpu.make_async_copy(src, dst, small_sem.at[n])
+        for n, (src, dst) in enumerate(
+            (
+                (dims_in, dims_ref),
+                (send_in, send_ref),
+                (recv_in, recv_ref),
+                (weight_in, weight_ref),
+                (cc_in, cc_ref),
+                (pp_in, pp_v),
+            )
+        )
+    ]
+    for copy in small:
+        copy.start()
     barrier = pltpu.get_barrier_semaphore()
 
     def greet(step, _):
@@ -72,12 +85,14 @@
     lax.fori_loop(1, PEERS, greet, 0)
     pl.semaphore_signal(barrier, inc=1, device_id={"row": other}, device_id_type=MESH)
 
+    for copy in small[:2]:
+        copy.wait()
     limit = dims_ref[slot_ref[0]]
 
     def live(i, k):
         row_ids = row * ROWS + i * PAIR + lax.broadcasted_iota(jnp.int32, (PAIR, COLT), 0)
-        col_ids = k * COLT + lax.broadcasted_iota(jnp.int32, (PAIR, COLT), 1)
-        return (row_ids < limit) & (col_ids < limit)
+        col_ids = k * COLT + lax.broadcasted_iota(jnp.int32, (1, COLT), 1)
+        return row_ids < jnp.where(col_ids < limit, limit, 0)
 
     def prologue(i, _):
         load(i, False)
@@ -96,13 +111,11 @@
         return 0
 
     lax.fori_loop(0, PAIRS, prologue, 0)
-    new_copy = pltpu.make_async_copy(mag_v, new_out.at[0], new_sem)
-    new_copy.start()
     pl.semaphore_wait(barrier, PEERS)
 
     def pick(to):
         for l in range(SLOTS):
-            tile = jnp.minimum(send_ref[0, to, l], TILES - 1)
+            tile = jnp.minimum(send_ref[l, 0, to], TILES - 1)
             sbuf[to * SLOTS + l] = stack[tile]
 
     def message(step):
@@ -110,7 +123,7 @@
         return pltpu.make_async_remote_copy(
             sbuf.at[pl.ds(to * SLOTS, SLOTS)],
             near.at[pl.ds(me * SLOTS, SLOTS)],
-            send_sem.at[step],
+            send_sem,
             recv_sem.at[step],
             device_id={"chan": to},
             device_id_type=MESH,
@@ -121,7 +134,7 @@
         return pltpu.make_async_remote_copy(
             sbuf.at[pl.ds(fr * SLOTS, SLOTS)],
             near.at[pl.ds(fr * SLOTS, SLOTS)],
-            send_sem.at[step],
+            send_sem,
             recv_sem.at[step],
             device_id={"chan": fr},
             device_id_type=MESH,
@@ -130,7 +143,7 @@
     def handed(step):
         at = pl.ds(spin(me, step, -1) * SLOTS, SLOTS)
         return pltpu.make_async_remote_copy(
-            near.at[at], far.at[at], hand_sem.at[step], take_sem.at[step],
+            near.at[at], far.at[at], hand_sem, take_sem,
             device_id={"row": other}, device_id_type=MESH,
         )
 
@@ -146,7 +159,8 @@
     )
     mine.start()
 
-    pp_copy.wait()
+    for copy in small[2:]:
+        copy.wait()
     chosen = lax.broadcasted_iota(jnp.int32, pp_v.shape, 0) == slot_ref[0]
     factor = jnp.sum(jnp.where(chosen, pp_v[...], 0.0), axis=0, keepdims=True)
 
@@ -188,7 +202,7 @@
 
     def invert_send(d, table):
         for l in range(SLOTS):
-            table = jnp.where(place == send_ref[0, d, l], d * SLOTS + l, table)
+            table = jnp.where(place == send_ref[l, 0, d], d * SLOTS + l, table)
         return table
 
     blank = jnp.zeros((8, COLT), jnp.int32)
@@ -201,15 +215,9 @@
         strip(which, other).wait_recv()
         strip(which, row).wait_send()
 
-    def pp_product(n, _):
-        col = pl.ds(pl.multiple_of(n * CHUNK, CHUNK), CHUNK)
-        part = jnp.dot(left[...], right[:, col], preferred_element_type=F32)
-        for half in range(CHUNK // COLT):
-            at = rows_at((n * (CHUNK // COLT) + half) * ROWS, ROWS, 8)
-            base[at, :] += part[:, half * COLT : (half + 1) * COLT]
-        return 0
-
-    lax.fori_loop(0, WIDTH // CHUNK, pp_product, 0)
+    part = jnp.dot(left[...], right[...], preferred_element_type=F32)
+    for k in range(BLOCKS):
+        base[pl.ds(k * ROWS, ROWS), :] += part[:, k * COLT : (k + 1) * COLT]
     inv_copy.wait()
 
     def hand_on(step, _):
@@ -245,23 +253,16 @@
 
     settle(near, row, True)
 
-    def take(step, _):
-        handed(step).wait_recv()
-        return 0
-
-    lax.fori_loop(0, PEERS, take, 0)
+    all_handed = pltpu.make_async_remote_copy(
+        near, far, hand_sem, take_sem, device_id={"row": other}, device_id_type=MESH
+    )
+    all_handed.wait_recv()
     settle(far, other, False)
 
-    def cc_product(n, _):
-        col = pl.ds(pl.multiple_of(n * CHUNK, CHUNK), CHUNK)
-        part = jnp.dot(left[...], right[:, col], preferred_element_type=F32)
-        for half in range(CHUNK // COLT):
-            for a in range(ROWS // TR):
-                tile = a * BLOCKS + n * (CHUNK // COLT) + half
-                cross[tile] = part[a * TR : (a + 1) * TR, half * COLT : (half + 1) * COLT]
-        return 0
-
-    lax.fori_loop(0, WIDTH // CHUNK, cc_product, 0)
+    part = jnp.dot(left[...], right[...], preferred_element_type=F32)
+    for a in range(ROWS // TR):
+        for k in range(BLOCKS):
+            cross[a * BLOCKS + k] = part[a * TR : (a + 1) * TR, k * COLT : (k + 1) * COLT]
 
     def pick_back(to):
         parts = []
@@ -277,7 +278,7 @@
         return pltpu.make_async_remote_copy(
             tsend.at[rows_at(to * BACK, BACK, 16)],
             trecv.at[rows_at(me * BACK, BACK, 16)],
-            bsend_sem.at[step],
+            bsend_sem,
             brecv_sem.at[step],
             device_id={"chan": to},
             device_id_type=MESH,
@@ -288,7 +289,7 @@
         return pltpu.make_async_remote_copy(
             tsend.at[rows_at(fr * BACK, BACK, 16)],
             trecv.at[rows_at(fr * BACK, BACK, 16)],
-            bsend_sem.at[step],
+            bsend_sem,
             brecv_sem.at[step],
             device_id={"chan": fr},
             device_id_type=MESH,
@@ -333,42 +334,51 @@
                 u = (2 * i + half) * BLOCKS + k
                 slot = inv_s[1, lax.div(u, COLT), lax.rem(u, COLT)]
                 parts.append(unpacked[slot])
-            total = base[rows_at(k * ROWS + i * PAIR, PAIR, 8), :] + jnp.concatenate(parts, axis=0)
-            gen_v[at, pl.ds(k * COLT, COLT)] = jnp.where(live(i, k), total, 0.0).astype(BF16)
+            back_part = jnp.where(live(i, k), jnp.concatenate(parts, axis=0), 0.0)
+            total = base[rows_at(k * ROWS + i * PAIR, PAIR, 8), :] + back_part
+            gen_v[at, pl.ds(k * COLT, COLT)] = total.astype(BF16)
         out_copy(i).start()
         return 0
 
     lax.fori_loop(0, PAIRS, finish, 0)
 
-    def drain(step, _):
-        message(step).wait_send()
-        handed(step).wait_send()
-        back(step).wait_send()
-        return 0
-
-    lax.fori_loop(1, PEERS, drain, 0)
-    handed(0).wait_send()
-    new_copy.wait()
+    out_total = pl.ds(0, (PEERS - 1) * SLOTS)
+    pltpu.make_async_remote_copy(
+        sbuf.at[out_total], near.at[out_total], send_sem, recv_sem.at[0],
+        device_id={"row": other}, device_id_type=MESH,
+    ).wait_send()
+    all_handed.wait_send()
+    back_total = pl.ds(0, (PEERS - 1) * BACK)
+    pltpu.make_async_remote_copy(
+        tsend.at[back_total], trecv.at[back_total], bsend_sem, brecv_sem.at[0],
+        device_id={"row": other}, device_id_type=MESH,
+    ).wait_send()
     for i in range(PAIRS):
         out_copy(i).wait()
 
 
-def per_device(*args):
-    strip = jax.ShapeDtypeStruct(args[0].shape, BF16)
+def per_device(gen, mag, ham, slot, dims, pp, cc, send, recv, weight):
+    strip = jax.ShapeDtypeStruct(gen.shape, BF16)
+    magnus_new = (mag.astype(F32) + STEP_SIZE * gen.astype(F32)).astype(BF16)
+    args = (gen, mag, ham, slot, dims, pp, cc, send.transpose(2, 0, 1), recv, weight)
     hbm = pl.BlockSpec(memory_space=pltpu.HBM)
-    smem = pl.BlockSpec(memory_space=pltpu.SMEM)
-    vmem = pl.BlockSpec(memory_space=pltpu.VMEM)
     dma = pltpu.SemaphoreType.DMA
-    return pl.pallas_call(
+    flowed = pl.pallas_call(
         kernel,
-        out_shape=(strip, strip),
-        in_specs=[hbm, hbm, hbm, smem, smem, hbm, vmem, smem, smem, smem],
-        out_specs=(hbm, hbm),
+        out_shape=strip,
+        in_specs=[hbm] * 3 + [pl.BlockSpec(memory_space=pltpu.SMEM)] + [hbm] * 6,
+        out_specs=hbm,
         scratch_shapes=[
+            pltpu.SMEM(dims.shape, jnp.int32),
+            pltpu.VMEM(pp.shape, F32),
+            pltpu.VMEM(cc.shape, F32),
+            pltpu.SMEM(args[7].shape, jnp.int32),
+            pltpu.SMEM(recv.shape, jnp.int32),
+            pltpu.SMEM(weight.shape, F32),
+            dma((6,)),
             pltpu.VMEM((ROWS, WIDTH), BF16),
             pltpu.VMEM((ROWS, WIDTH), BF16),
             pltpu.VMEM((ROWS, WIDTH), BF16),
-            pltpu.VMEM((PEERS, WIDTH), F32),
             pltpu.VMEM((TILES, PAIR, COLT), BF16),
             pltpu.VMEM((PEERS * SLOTS, PAIR, COLT), BF16),
             pltpu.VMEM((PEERS * SLOTS, PAIR, COLT), BF16),
@@ -384,17 +394,15 @@
             pltpu.SMEM((2, 8, COLT), jnp.int32),
             dma((3, PAIRS)),
             dma,
-            dma,
             dma((PAIRS,)),
             dma,
             dma,
             dma((PEERS,)),
-            dma((PEERS,)),
-            dma((PEERS,)),
-            dma((PEERS,)),
+            dma,
+            dma,
             dma((2,)),
             dma((2,)),
-            dma((PEERS,)),
+            dma,
             dma((PEERS,)),
             dma,
         ],
@@ -402,6 +410,7 @@
             collective_id=0, has_side_effects=True, vmem_limit_bytes=58 << 20
         ),
     )(*args)
+    return magnus_new, flowed
 
 
 def solution(mesh):

time: 106 us -> 99.3 us (0.937)
  local copies, waits for them, and re-layouts: 5.37 us -> 1.18 us
  Pallas kernels: 98.8 us -> 95 us
  other arithmetic: 0 us -> 1.65 us
    unnamed x5 -> x7, local copies, waits for them, and re-layouts: 5.37 us -> 1.18 us
    pallas_call x1, Pallas kernels: 98.8 us -> 95 us  [per_device(): pl.pallas_call(kernel, out_shape=strip, in_specs=[hbm] * 3 + [pl.BlockSpe...]
    convert_element_type x0 -> x1, other arithmetic: none -> 1.65 us  [per_device(): magnus_new = (mag.astype(F32) + STEP_SIZE * gen.astype(F32)).astype(BF16)]
where the time goes in v2:
time: 99.3 us; the launch traced here: 99.2 us
  Pallas kernels  95 us (96%)
  other arithmetic  1.65 us (2%)
  between operations  1.33 us (1%)
  local copies, waits for them, and re-layouts  1.18 us (1%)
    pallas_call x1, Pallas kernels, per_device(): pl.pallas_call(kernel, out_shape=strip, in_specs=[hbm] * 3 + [pl.BlockSpe...  95 us

profile of v2, /device:TPU:0, one launch (start us, length us, event | category | flops | bytes accessed | tf_op | source)
XLA Modules:
  0.0 99.2 jit_solution(8987167629933675819)
XLA Ops:
  1.3 0.0 copy-start
  1.3 0.0 copy-start.1
  1.3 95.0 %shard_map.113 = bf16[1,640,1280]{2,1,0:T(8,128)(2,1)} custom-call(bf16[1,640,1280]{2,1,0:T(8,128)(2,1)} %gen.1, bf16[1,640,1280]{2,1,0:T(8,128)(2,1)} %mag.1, bf16[1,640,1280]{2,1,0:T(8,128)(2,1)} %ham.1, s32[1]{0:T(128)S(6)} %copy.13.slot_ref, s32[64]{0:T(128)} %dims_in.1, f32[64,1280]{1,0:T(8,128)} %pp_in.1, f32[1,1280]{1,0:T(1,128)} %cc_in.1, ...), custom_call_target="tpu_custom_call" | custom-call | tf_op jit(solution)/shard_map/pallas_call | solution.py:366
  96.3 0.0 copy-done
  96.3 0.0 copy-done.1
  96.3 0.0 copy-start.2
  96.3 1.7 %add_convert_fusion = bf16[1,640,1280]{2,1,0:T(8,128)(2,1)} fusion(bf16[1,640,1280]{2,1,0:T(8,128)(2,1)S(1)} %copy-done, bf16[1,640,1280]{2,1,0:T(8,128)(2,1)S(1)} %copy-done.1), kind=kLoop, calls=%fused_computation | loop fusion | flops 4096000 | bytes 4915200 | tf_op jit(solution)/shard_map/convert_element_type | solution.py:362
  98.0 0.0 copy-done.2
  98.0 1.2 %copy.14 = bf16[1,640,1280]{2,1,0:T(8,128)(2,1)} copy(bf16[1,640,1280]{2,1,0:T(8,128)(2,1)S(1)} %copy-done.2) | data formatting | bytes 3276800
Async XLA Ops:
  1.3 95.0 %copy-start = (bf16[1,640,1280]{2,1,0:T(8,128)(2,1)S(1)}, bf16[1,640,1280]{2,1,0:T(8,128)(2,1)}, u32[]{:S(2)}) copy-start(bf16[1,640,1280]{2,1,0:T(8,128)(2,1)} %gen.1) | copy-start | bytes 4915204
  1.3 95.0 %copy-start.1 = (bf16[1,640,1280]{2,1,0:T(8,128)(2,1)S(1)}, bf16[1,640,1280]{2,1,0:T(8,128)(2,1)}, u32[]{:S(2)}) copy-start(bf16[1,640,1280]{2,1,0:T(8,128)(2,1)} %mag.1) | copy-start | bytes 4915204
  96.3 1.7 %copy-start.2 = (bf16[1,640,1280]{2,1,0:T(8,128)(2,1)S(1)}, bf16[1,640,1280]{2,1,0:T(8,128)(2,1)}, u32[]{:S(2)}) copy-start(bf16[1,640,1280]{2,1,0:T(8,128)(2,1)} %shard_map.113) | copy-start | bytes 4915204

commit v3 on v2

--- a/solution.py
+++ b/solution.py
@@ -23,7 +23,6 @@
 PAIRS = ROWS // (2 * TR)
 TILES = (ROWS // TR) * BLOCKS
 PAIR = 2 * TR
-BACK = 128
 
 
 def spin(me, step, sign):
@@ -42,7 +41,7 @@
     gen, mag, ham, slot_ref, dims_in, pp_in, cc_in, send_in, recv_in, weight_in,
     flow_out,
     dims_ref, pp_v, cc_ref, send_ref, recv_ref, weight_ref, small_sem,
-    gen_v, mag_v, ham_v, stack, sbuf, near, far, right, left, base, cross, tsend, trecv, unpacked,
+    gen_v, mag_v, ham_v, stack, sbuf, near, far, right, left, base, cross, tsend, trecv,
     inv_v, inv_s,
     in_sem, inv_sem, out_sem, self_sem, send_sem, recv_sem, hand_sem, take_sem,
     strip_send, strip_recv, bsend_sem, brecv_sem, bself_sem,
@@ -78,7 +77,7 @@
 
     def greet(step, _):
         pl.semaphore_signal(
-            barrier, inc=1, device_id={"chan": spin(me, step, 1)}, device_id_type=MESH
+            barrier, inc=1, device_id={"chan": lax.rem(me + step, PEERS)}, device_id_type=MESH
         )
         return 0
 
@@ -265,19 +264,16 @@
             cross[a * BLOCKS + k] = part[a * TR : (a + 1) * TR, k * COLT : (k + 1) * COLT]
 
     def pick_back(to):
-        parts = []
         for l in range(SLOTS):
             slot = to * SLOTS + l
             v = inv_s[0, lax.div(slot, COLT), lax.rem(slot, COLT)]
-            parts.append(weight_ref[0, v] * cross[v])
-        parts.append(jnp.zeros((BACK - SLOTS * TR, COLT), F32))
-        tsend[rows_at(to * BACK, BACK, 16), :] = jnp.concatenate(parts, axis=0).astype(BF16)
+            tsend[slot] = (weight_ref[0, v] * cross[v]).astype(BF16)
 
     def back(step):
         to = spin(me, step, 1)
         return pltpu.make_async_remote_copy(
-            tsend.at[rows_at(to * BACK, BACK, 16)],
-            trecv.at[rows_at(me * BACK, BACK, 16)],
+            tsend.at[pl.ds(to * SLOTS, SLOTS)],
+            trecv.at[pl.ds(me * SLOTS, SLOTS)],
             bsend_sem,
             brecv_sem.at[step],
             device_id={"chan": to},
@@ -287,8 +283,8 @@
     def back_arrival(step):
         fr = spin(me, step, -1)
         return pltpu.make_async_remote_copy(
-            tsend.at[rows_at(fr * BACK, BACK, 16)],
-            trecv.at[rows_at(fr * BACK, BACK, 16)],
+            tsend.at[pl.ds(fr * SLOTS, SLOTS)],
+            trecv.at[pl.ds(fr * SLOTS, SLOTS)],
             bsend_sem,
             brecv_sem.at[step],
             device_id={"chan": fr},
@@ -303,21 +299,14 @@
     lax.fori_loop(1, PEERS, send_back, 0)
     pick_back(me)
     home = pltpu.make_async_copy(
-        tsend.at[rows_at(me * BACK, BACK, 16)], trecv.at[rows_at(me * BACK, BACK, 16)], bself_sem
+        tsend.at[pl.ds(me * SLOTS, SLOTS)], trecv.at[pl.ds(me * SLOTS, SLOTS)], bself_sem
     )
     home.start()
 
-    def unpack(fr):
-        rows = trecv[rows_at(fr * BACK, BACK, 16), :].astype(F32)
-        for l in range(SLOTS):
-            unpacked[fr * SLOTS + l] = rows[l * TR : (l + 1) * TR]
-
     home.wait()
-    unpack(me)
 
     def take_back(step, _):
         back_arrival(step).wait_recv()
-        unpack(spin(me, step, -1))
         return 0
 
     lax.fori_loop(1, PEERS, take_back, 0)
@@ -333,7 +322,7 @@
             for half in range(2):
                 u = (2 * i + half) * BLOCKS + k
                 slot = inv_s[1, lax.div(u, COLT), lax.rem(u, COLT)]
-                parts.append(unpacked[slot])
+                parts.append(trecv[slot].astype(F32))
             back_part = jnp.where(live(i, k), jnp.concatenate(parts, axis=0), 0.0)
             total = base[rows_at(k * ROWS + i * PAIR, PAIR, 8), :] + back_part
             gen_v[at, pl.ds(k * COLT, COLT)] = total.astype(BF16)
@@ -348,7 +337,7 @@
         device_id={"row": other}, device_id_type=MESH,
     ).wait_send()
     all_handed.wait_send()
-    back_total = pl.ds(0, (PEERS - 1) * BACK)
+    back_total = out_total
     pltpu.make_async_remote_copy(
         tsend.at[back_total], trecv.at[back_total], bsend_sem, brecv_sem.at[0],
         device_id={"row": other}, device_id_type=MESH,
@@ -387,9 +376,8 @@
             pltpu.VMEM((ROWS, 2 * WIDTH), BF16),
             pltpu.VMEM((BLOCKS * ROWS, COLT), F32),
             pltpu.VMEM((TILES, TR, COLT), F32),
-            pltpu.VMEM((PEERS * BACK, COLT), BF16),
-            pltpu.VMEM((PEERS * BACK, COLT), BF16),
-            pltpu.VMEM((PEERS * SLOTS, TR, COLT), F32),
+            pltpu.VMEM((PEERS * SLOTS, TR, COLT), BF16),
+            pltpu.VMEM((PEERS * SLOTS, TR, COLT), BF16),
             pltpu.VMEM((2, 8, COLT), jnp.int32),
             pltpu.SMEM((2, 8, COLT), jnp.int32),
             dma((3, PAIRS)),

time: 99.3 us -> 96.9 us (0.976)
  Pallas kernels: 95 us -> 92.1 us
    pallas_call x1, Pallas kernels: 95 us -> 92.1 us  [per_device(): pl.pallas_call(kernel, out_shape=strip, in_specs=[hbm] * 3 + [pl.BlockSpe...]
where the time goes in v3:
time: 96.9 us; the launch traced here: 96.3 us
  Pallas kernels  92.1 us (95%)
  other arithmetic  1.65 us (2%)
  between operations  1.33 us (1%)
  local copies, waits for them, and re-layouts  1.18 us (1%)
    pallas_call x1, Pallas kernels, per_device(): pl.pallas_call(kernel, out_shape=strip, in_specs=[hbm] * 3 + [pl.BlockSpe...  92.1 us

profile of v3, /device:TPU:0, one launch (start us, length us, event | category | flops | bytes accessed | tf_op | source)
XLA Modules:
  0.0 96.3 jit_solution(3180429806728352584)
XLA Ops:
  1.3 0.0 copy-start
  1.3 0.0 copy-start.1
  1.3 92.1 %shard_map.113 = bf16[1,640,1280]{2,1,0:T(8,128)(2,1)} custom-call(bf16[1,640,1280]{2,1,0:T(8,128)(2,1)} %gen.1, bf16[1,640,1280]{2,1,0:T(8,128)(2,1)} %mag.1, bf16[1,640,1280]{2,1,0:T(8,128)(2,1)} %ham.1, s32[1]{0:T(128)S(6)} %copy.13.slot_ref, s32[64]{0:T(128)} %dims_in.1, f32[64,1280]{1,0:T(8,128)} %pp_in.1, f32[1,1280]{1,0:T(1,128)} %cc_in.1, ...), custom_call_target="tpu_custom_call" | custom-call | tf_op jit(solution)/shard_map/pallas_call | solution.py:355
  93.4 0.0 copy-done
  93.4 0.0 copy-done.1
  93.4 0.0 copy-start.2
  93.5 1.7 %add_convert_fusion = bf16[1,640,1280]{2,1,0:T(8,128)(2,1)} fusion(bf16[1,640,1280]{2,1,0:T(8,128)(2,1)S(1)} %copy-done, bf16[1,640,1280]{2,1,0:T(8,128)(2,1)S(1)} %copy-done.1), kind=kLoop, calls=%fused_computation | loop fusion | flops 4096000 | bytes 4915200 | tf_op jit(solution)/shard_map/convert_element_type | solution.py:351
  95.1 0.0 copy-done.2
  95.1 1.2 %copy.14 = bf16[1,640,1280]{2,1,0:T(8,128)(2,1)} copy(bf16[1,640,1280]{2,1,0:T(8,128)(2,1)S(1)} %copy-done.2) | data formatting | bytes 3276800
Async XLA Ops:
  1.3 92.1 %copy-start = (bf16[1,640,1280]{2,1,0:T(8,128)(2,1)S(1)}, bf16[1,640,1280]{2,1,0:T(8,128)(2,1)}, u32[]{:S(2)}) copy-start(bf16[1,640,1280]{2,1,0:T(8,128)(2,1)} %gen.1) | copy-start | bytes 4915204
  1.3 92.1 %copy-start.1 = (bf16[1,640,1280]{2,1,0:T(8,128)(2,1)S(1)}, bf16[1,640,1280]{2,1,0:T(8,128)(2,1)}, u32[]{:S(2)}) copy-start(bf16[1,640,1280]{2,1,0:T(8,128)(2,1)} %mag.1) | copy-start | bytes 4915204
  93.4 1.7 %copy-start.2 = (bf16[1,640,1280]{2,1,0:T(8,128)(2,1)S(1)}, bf16[1,640,1280]{2,1,0:T(8,128)(2,1)}, u32[]{:S(2)}) copy-start(bf16[1,640,1280]{2,1,0:T(8,128)(2,1)} %shard_map.113) | copy-start | bytes 4915204

commit v4 on v3

--- a/solution.py
+++ b/solution.py
@@ -22,6 +22,8 @@
 BLOCKS = WIDTH // COLT
 PAIRS = ROWS // (2 * TR)
 TILES = (ROWS // TR) * BLOCKS
+HEAD = 16
+REST = TR - HEAD
 PAIR = 2 * TR
 
 
@@ -41,7 +43,7 @@
     gen, mag, ham, slot_ref, dims_in, pp_in, cc_in, send_in, recv_in, weight_in,
     flow_out,
     dims_ref, pp_v, cc_ref, send_ref, recv_ref, weight_ref, small_sem,
-    gen_v, mag_v, ham_v, stack, sbuf, near, far, right, left, base, cross, tsend, trecv,
+    gen_v, mag_v, ham_v, stack, sbuf, near, far, right, left, base, cross_a, cross_b, tsend_a, tsend_b, trecv_a, trecv_b,
     inv_v, inv_s,
     in_sem, inv_sem, out_sem, self_sem, send_sem, recv_sem, hand_sem, take_sem,
     strip_send, strip_recv, bsend_sem, brecv_sem, bself_sem,
@@ -243,9 +245,16 @@
                 right[under, col] = m.astype(BF16)
                 if own:
                     f = cc_ref[:, k * COLT : (k + 1) * COLT]
-                    here = rows_at(i * PAIR, PAIR, 16)
-                    left[here, col] = (m * f).astype(BF16)
-                    left[here, pl.ds(WIDTH + k * COLT, COLT)] = (h * -f).astype(BF16)
+                    first = rows_at(i * 2 * HEAD, 2 * HEAD, 16)
+                    second = rows_at(ROWS // TR * HEAD + i * 2 * REST, 2 * REST, 16)
+                    for value, place in ((m * f, k * COLT), (h * -f, WIDTH + k * COLT)):
+                        side = pl.ds(place, COLT)
+                        left[first, side] = jnp.concatenate(
+                            [value[:HEAD], value[TR : TR + HEAD]], axis=0
+                        ).astype(BF16)
+                        left[second, side] = jnp.concatenate(
+                            [value[HEAD:TR], value[TR + HEAD :]], axis=0
+                        ).astype(BF16)
             return 0
 
         lax.fori_loop(0, PAIRS, body, 0)
@@ -258,58 +267,50 @@
     all_handed.wait_recv()
     settle(far, other, False)
 
-    part = jnp.dot(left[...], right[...], preferred_element_type=F32)
-    for a in range(ROWS // TR):
-        for k in range(BLOCKS):
-            cross[a * BLOCKS + k] = part[a * TR : (a + 1) * TR, k * COLT : (k + 1) * COLT]
-
-    def pick_back(to):
+    def product(start, size, cross):
+        rows = left[start : start + size * (ROWS // TR), :]
+        part = jnp.dot(rows, right[...], preferred_element_type=F32)
+        for a in range(ROWS // TR):
+            for k in range(BLOCKS):
+                cross[a * BLOCKS + k] = part[a * size : (a + 1) * size, k * COLT : (k + 1) * COLT]
+
+    def pick_back(to, cross, tsend):
         for l in range(SLOTS):
             slot = to * SLOTS + l
             v = inv_s[0, lax.div(slot, COLT), lax.rem(slot, COLT)]
             tsend[slot] = (weight_ref[0, v] * cross[v]).astype(BF16)
 
-    def back(step):
-        to = spin(me, step, 1)
-        return pltpu.make_async_remote_copy(
-            tsend.at[pl.ds(to * SLOTS, SLOTS)],
-            trecv.at[pl.ds(me * SLOTS, SLOTS)],
-            bsend_sem,
-            brecv_sem.at[step],
-            device_id={"chan": to},
-            device_id_type=MESH,
-        )
-
-    def back_arrival(step):
-        fr = spin(me, step, -1)
-        return pltpu.make_async_remote_copy(
-            tsend.at[pl.ds(fr * SLOTS, SLOTS)],
-            trecv.at[pl.ds(fr * SLOTS, SLOTS)],
-            bsend_sem,
-            brecv_sem.at[step],
-            device_id={"chan": fr},
-            device_id_type=MESH,
-        )
-
-    def send_back(step, _):
-        pick_back(spin(me, step, 1))
-        back(step).start()
-        return 0
-
-    lax.fori_loop(1, PEERS, send_back, 0)
-    pick_back(me)
-    home = pltpu.make_async_copy(
-        tsend.at[pl.ds(me * SLOTS, SLOTS)], trecv.at[pl.ds(me * SLOTS, SLOTS)], bself_sem
-    )
-    home.start()
-
-    home.wait()
-
-    def take_back(step, _):
-        back_arrival(step).wait_recv()
-        return 0
-
-    lax.fori_loop(1, PEERS, take_back, 0)
+    mine_at = pl.ds(me * SLOTS, SLOTS)
+    parts_back = ((0, HEAD, cross_a, tsend_a, trecv_a), (ROWS // TR * HEAD, REST, cross_b, tsend_b, trecv_b))
+    homes = []
+    for n, (start, size, cross, tsend, trecv) in enumerate(parts_back):
+        product(start, size, cross)
+
+        def send_back(step, _):
+            to = spin(me, step, 1)
+            pick_back(to, cross, tsend)
+            pltpu.make_async_remote_copy(
+                tsend.at[pl.ds(to * SLOTS, SLOTS)], trecv.at[mine_at], bsend_sem.at[n], brecv_sem.at[n],
+                device_id={"chan": to}, device_id_type=MESH,
+            ).start()
+            return 0
+
+        lax.fori_loop(1, PEERS, send_back, 0)
+        pick_back(me, cross, tsend)
+        homes.append(pltpu.make_async_copy(tsend.at[mine_at], trecv.at[mine_at], bself_sem.at[n]))
+        homes[n].start()
+
+    others = pl.ds(0, (PEERS - 1) * SLOTS)
+    all_back = [
+        pltpu.make_async_remote_copy(
+            tsend.at[others], trecv.at[others], bsend_sem.at[n], brecv_sem.at[n],
+            device_id={"row": other}, device_id_type=MESH,
+        )
+        for n, (_, _, _, tsend, trecv) in enumerate(parts_back)
+    ]
+    for n in range(2):
+        homes[n].wait()
+        all_back[n].wait_recv()
 
     def out_copy(i):
         at = rows_at(i * PAIR, PAIR, 16)
@@ -322,7 +323,7 @@
             for half in range(2):
                 u = (2 * i + half) * BLOCKS + k
                 slot = inv_s[1, lax.div(u, COLT), lax.rem(u, COLT)]
-                parts.append(trecv[slot].astype(F32))
+                parts += [trecv_a[slot].astype(F32), trecv_b[slot].astype(F32)]
             back_part = jnp.where(live(i, k), jnp.concatenate(parts, axis=0), 0.0)
             total = base[rows_at(k * ROWS + i * PAIR, PAIR, 8), :] + back_part
             gen_v[at, pl.ds(k * COLT, COLT)] = total.astype(BF16)
@@ -331,17 +332,13 @@
 
     lax.fori_loop(0, PAIRS, finish, 0)
 
-    out_total = pl.ds(0, (PEERS - 1) * SLOTS)
     pltpu.make_async_remote_copy(
-        sbuf.at[out_total], near.at[out_total], send_sem, recv_sem.at[0],
+        sbuf.at[others], near.at[others], send_sem, recv_sem.at[0],
         device_id={"row": other}, device_id_type=MESH,
     ).wait_send()
     all_handed.wait_send()
-    back_total = out_total
-    pltpu.make_async_remote_copy(
-        tsend.at[back_total], trecv.at[back_total], bsend_sem, brecv_sem.at[0],
-        device_id={"row": other}, device_id_type=MESH,
-    ).wait_send()
+    for n in range(2):
+        all_back[n].wait_send()
     for i in range(PAIRS):
         out_copy(i).wait()
 
@@ -375,9 +372,12 @@
             pltpu.VMEM((2 * WIDTH, WIDTH), BF16),
             pltpu.VMEM((ROWS, 2 * WIDTH), BF16),
             pltpu.VMEM((BLOCKS * ROWS, COLT), F32),
-            pltpu.VMEM((TILES, TR, COLT), F32),
-            pltpu.VMEM((PEERS * SLOTS, TR, COLT), BF16),
-            pltpu.VMEM((PEERS * SLOTS, TR, COLT), BF16),
+            pltpu.VMEM((TILES, HEAD, COLT), F32),
+            pltpu.VMEM((TILES, REST, COLT), F32),
+            pltpu.VMEM((PEERS * SLOTS, HEAD, COLT), BF16),
+            pltpu.VMEM((PEERS * SLOTS, REST, COLT), BF16),
+            pltpu.VMEM((PEERS * SLOTS, HEAD, COLT), BF16),
+            pltpu.VMEM((PEERS * SLOTS, REST, COLT), BF16),
             pltpu.VMEM((2, 8, COLT), jnp.int32),
             pltpu.SMEM((2, 8, COLT), jnp.int32),
             dma((3, PAIRS)),
@@ -390,9 +390,9 @@
             dma,
             dma((2,)),
             dma((2,)),
-            dma,
-            dma((PEERS,)),
-            dma,
+            dma((2,)),
+            dma((2,)),
+            dma((2,)),
         ],
         compiler_params=pltpu.CompilerParams(
             collective_id=0, has_side_effects=True, vmem_limit_bytes=58 << 20

time: 96.9 us -> 93.9 us (0.969)
  Pallas kernels: 92.1 us -> 89.2 us
    pallas_call x1, Pallas kernels: 92.1 us -> 89.2 us  [per_device(): pl.pallas_call(kernel, out_shape=strip, in_specs=[hbm] * 3 + [pl.BlockSpe...]
where the time goes in v4:
time: 93.9 us; the launch traced here: 93.3 us
  Pallas kernels  89.2 us (95%)
  other arithmetic  1.65 us (2%)
  between operations  1.33 us (1%)
  local copies, waits for them, and re-layouts  1.18 us (1%)
    pallas_call x1, Pallas kernels, per_device(): pl.pallas_call(kernel, out_shape=strip, in_specs=[hbm] * 3 + [pl.BlockSpe...  89.2 us

profile of v4, /device:TPU:0, one launch (start us, length us, event | category | flops | bytes accessed | tf_op | source)
XLA Modules:
  0.0 93.3 jit_solution(12802081232131252105)
XLA Ops:
  1.3 0.0 copy-start
  1.3 0.0 copy-start.1
  1.3 89.2 %shard_map.113 = bf16[1,640,1280]{2,1,0:T(8,128)(2,1)} custom-call(bf16[1,640,1280]{2,1,0:T(8,128)(2,1)} %gen.1, bf16[1,640,1280]{2,1,0:T(8,128)(2,1)} %mag.1, bf16[1,640,1280]{2,1,0:T(8,128)(2,1)} %ham.1, s32[1]{0:T(128)S(6)} %copy.13.slot_ref, s32[64]{0:T(128)} %dims_in.1, f32[64,1280]{1,0:T(8,128)} %pp_in.1, f32[1,1280]{1,0:T(1,128)} %cc_in.1, ...), custom_call_target="tpu_custom_call" | custom-call | tf_op jit(solution)/shard_map/pallas_call | solution.py:352
  90.5 0.0 copy-done
  90.5 0.0 copy-done.1
  90.5 0.0 copy-start.2
  90.5 1.7 %add_convert_fusion = bf16[1,640,1280]{2,1,0:T(8,128)(2,1)} fusion(bf16[1,640,1280]{2,1,0:T(8,128)(2,1)S(1)} %copy-done, bf16[1,640,1280]{2,1,0:T(8,128)(2,1)S(1)} %copy-done.1), kind=kLoop, calls=%fused_computation | loop fusion | flops 4096000 | bytes 4915200 | tf_op jit(solution)/shard_map/convert_element_type | solution.py:348
  92.2 0.0 copy-done.2
  92.2 1.2 %copy.14 = bf16[1,640,1280]{2,1,0:T(8,128)(2,1)} copy(bf16[1,640,1280]{2,1,0:T(8,128)(2,1)S(1)} %copy-done.2) | data formatting | bytes 3276800
Async XLA Ops:
  1.3 89.2 %copy-start = (bf16[1,640,1280]{2,1,0:T(8,128)(2,1)S(1)}, bf16[1,640,1280]{2,1,0:T(8,128)(2,1)}, u32[]{:S(2)}) copy-start(bf16[1,640,1280]{2,1,0:T(8,128)(2,1)} %gen.1) | copy-start | bytes 4915204
  1.3 89.2 %copy-start.1 = (bf16[1,640,1280]{2,1,0:T(8,128)(2,1)S(1)}, bf16[1,640,1280]{2,1,0:T(8,128)(2,1)}, u32[]{:S(2)}) copy-start(bf16[1,640,1280]{2,1,0:T(8,128)(2,1)} %mag.1) | copy-start | bytes 4915204
  90.5 1.7 %copy-start.2 = (bf16[1,640,1280]{2,1,0:T(8,128)(2,1)S(1)}, bf16[1,640,1280]{2,1,0:T(8,128)(2,1)}, u32[]{:S(2)}) copy-start(bf16[1,640,1280]{2,1,0:T(8,128)(2,1)} %shard_map.113) | copy-start | bytes 4915204

commit v5 on v4

--- a/solution.py
+++ b/solution.py
@@ -22,8 +22,13 @@
 BLOCKS = WIDTH // COLT
 PAIRS = ROWS // (2 * TR)
 TILES = (ROWS // TR) * BLOCKS
-HEAD = 16
+HEAD = 24
 REST = TR - HEAD
+EARLY = TR + HEAD
+STRIPES = ROWS // TR
+HEADS = 2 * STRIPES * HEAD
+LATE = HEADS + WIDTH
+LOADS = 4
 PAIR = 2 * TR
 
 
@@ -43,7 +48,8 @@
     gen, mag, ham, slot_ref, dims_in, pp_in, cc_in, send_in, recv_in, weight_in,
     flow_out,
     dims_ref, pp_v, cc_ref, send_ref, recv_ref, weight_ref, small_sem,
-    gen_v, mag_v, ham_v, stack, sbuf, near, far, right, left, base, cross_a, cross_b, tsend_a, tsend_b, trecv_a, trecv_b,
+    gen_v, mag_v, ham_v, stack, stack_late, sbuf, sbuf_late, near, near_late, far, far_late,
+    right, left, plain, perm, base, cross_a, cross_b, tsend_a, tsend_b, trecv_a, trecv_b,
     inv_v, inv_s,
     in_sem, inv_sem, out_sem, self_sem, send_sem, recv_sem, hand_sem, take_sem,
     strip_send, strip_recv, bsend_sem, brecv_sem, bself_sem,
@@ -52,14 +58,14 @@
     row = lax.axis_index("row")
     other = 1 - row
 
-    def load(i, start):
+    def load(part, start):
         for n, (src, dst) in enumerate(((gen, gen_v), (mag, mag_v), (ham, ham_v))):
-            at = rows_at(i * PAIR, PAIR, 16)
-            copy = pltpu.make_async_copy(src.at[0, at], dst.at[at], in_sem.at[n, i])
+            at = rows_at(part * (ROWS // LOADS), ROWS // LOADS, 16)
+            copy = pltpu.make_async_copy(src.at[0, at], dst.at[at], in_sem.at[n, part])
             copy.start() if start else copy.wait()
 
-    for i in range(PAIRS):
-        load(i, True)
+    for part in range(LOADS):
+        load(part, True)
     small = [
         pltpu.make_async_copy(src, dst, small_sem.at[n])
         for n, (src, dst) in enumerate(
@@ -95,8 +101,7 @@
         col_ids = k * COLT + lax.broadcasted_iota(jnp.int32, (1, COLT), 1)
         return row_ids < jnp.where(col_ids < limit, limit, 0)
 
-    def prologue(i, _):
-        load(i, False)
+    def cut(i):
         at = rows_at(i * PAIR, PAIR, 16)
         for k in range(BLOCKS):
             col = pl.ds(k * COLT, COLT)
@@ -105,60 +110,61 @@
             mask = live(i, k)
             m = jnp.where(mask, new.astype(F32), 0.0)
             h = jnp.where(mask, ham_v[at, col].astype(F32), 0.0)
-            for half in range(2):
-                cut = slice(half * TR, (half + 1) * TR)
-                tile = (2 * i + half) * BLOCKS + k
-                stack[tile] = jnp.concatenate([m[cut], h[cut]], axis=0).astype(BF16)
-        return 0
-
-    lax.fori_loop(0, PAIRS, prologue, 0)
+            for top in (0, TR):
+                tile = (2 * i + top // TR) * BLOCKS + k
+                stack[tile] = jnp.concatenate(
+                    [m[top : top + TR], h[top : top + HEAD]], axis=0
+                ).astype(BF16)
+                stack_late[tile] = h[top + HEAD : top + TR].astype(BF16)
+
+    def prologue(part, _):
+        load(part, False)
+        for sub in range(PAIRS // LOADS):
+            cut(part * (PAIRS // LOADS) + sub)
+        return 0
+
+    lax.fori_loop(0, LOADS, prologue, 0)
     pl.semaphore_wait(barrier, PEERS)
 
-    def pick(to):
+    waves = ((stack, sbuf, near, far), (stack_late, sbuf_late, near_late, far_late))
+
+    def slots_of(peer):
+        return pl.ds(peer * SLOTS, SLOTS)
+
+    def pick(to, tiles, out):
         for l in range(SLOTS):
             tile = jnp.minimum(send_ref[l, 0, to], TILES - 1)
-            sbuf[to * SLOTS + l] = stack[tile]
-
-    def message(step):
-        to = spin(me, step, 1)
+            out[to * SLOTS + l] = tiles[tile]
+
+    def message(wave, step, to, place):
+        _, out, held, _ = waves[wave]
         return pltpu.make_async_remote_copy(
-            sbuf.at[pl.ds(to * SLOTS, SLOTS)],
-            near.at[pl.ds(me * SLOTS, SLOTS)],
-            send_sem,
-            recv_sem.at[step],
-            device_id={"chan": to},
-            device_id_type=MESH,
-        )
-
-    def arrival(step):
-        fr = spin(me, step, -1)
+            out.at[slots_of(to)], held.at[slots_of(place)], send_sem.at[wave], recv_sem.at[wave, step],
+            device_id={"chan": to}, device_id_type=MESH,
+        )
+
+    def handed(wave, at):
+        _, _, held, passed = waves[wave]
         return pltpu.make_async_remote_copy(
-            sbuf.at[pl.ds(fr * SLOTS, SLOTS)],
-            near.at[pl.ds(fr * SLOTS, SLOTS)],
-            send_sem,
-            recv_sem.at[step],
-            device_id={"chan": fr},
-            device_id_type=MESH,
-        )
-
-    def handed(step):
-        at = pl.ds(spin(me, step, -1) * SLOTS, SLOTS)
-        return pltpu.make_async_remote_copy(
-            near.at[at], far.at[at], hand_sem, take_sem,
+            held.at[at], passed.at[at], hand_sem.at[wave], take_sem.at[wave],
             device_id={"row": other}, device_id_type=MESH,
         )
 
-    def send_out(step, _):
-        pick(spin(me, step, 1))
-        message(step).start()
-        return 0
-
-    lax.fori_loop(1, PEERS, send_out, 0)
-    pick(me)
-    mine = pltpu.make_async_copy(
-        sbuf.at[pl.ds(me * SLOTS, SLOTS)], near.at[pl.ds(me * SLOTS, SLOTS)], self_sem
-    )
-    mine.start()
+    mine = []
+    for wave, (tiles, out, held, _) in enumerate(waves):
+
+        def send_out(step, _):
+            to = spin(me, step, 1)
+            pick(to, tiles, out)
+            message(wave, step, to, me).start()
+            return 0
+
+        lax.fori_loop(1, PEERS, send_out, 0)
+        pick(me, tiles, out)
+        mine.append(
+            pltpu.make_async_copy(out.at[slots_of(me)], held.at[slots_of(me)], self_sem.at[wave])
+        )
+        mine[wave].start()
 
     for copy in small[2:]:
         copy.wait()
@@ -182,6 +188,22 @@
 
     lax.fori_loop(0, PAIRS, strips, 0)
 
+    def order(i, _):
+        at = rows_at(i * PAIR, PAIR, 16)
+        inside = lax.broadcasted_iota(jnp.int32, (PAIR, COLT), 0)
+        second = jnp.where(inside >= TR, 1, 0)
+        inside = inside - TR * second
+        stripe = 2 * i + second
+        target = jnp.where(
+            inside < HEAD, stripe * HEAD + inside, HEADS + stripe * REST + inside - HEAD
+        )
+        for k in range(BLOCKS):
+            ids = k * COLT + lax.broadcasted_iota(jnp.int32, (PAIR, COLT), 1)
+            perm[at, pl.ds(k * COLT, COLT)] = jnp.where(target == ids, 1.0, 0.0).astype(BF16)
+        return 0
+
+    lax.fori_loop(0, WIDTH // PAIR, order, 0)
+
     def strip(which, r):
         at = rows_at(which * WIDTH + r * ROWS, ROWS, 16)
         return pltpu.make_async_remote_copy(
@@ -191,8 +213,9 @@
 
     for which in range(2):
         strip(which, row).start()
-    mine.wait()
-    handed(0).start()
+    for wave in range(2):
+        mine[wave].wait()
+        handed(wave, slots_of(me)).start()
 
     place = lax.broadcasted_iota(jnp.int32, (8, COLT), 0) * COLT + lax.broadcasted_iota(
         jnp.int32, (8, COLT), 1
@@ -221,58 +244,83 @@
         base[pl.ds(k * ROWS, ROWS), :] += part[:, k * COLT : (k + 1) * COLT]
     inv_copy.wait()
 
-    def hand_on(step, _):
-        arrival(step).wait_recv()
-        handed(step).start()
-        return 0
-
-    lax.fori_loop(1, PEERS, hand_on, 0)
+    def hand_on(wave):
+        def body(step, _):
+            fr = spin(me, step, -1)
+            message(wave, step, fr, fr).wait_recv()
+            handed(wave, slots_of(fr)).start()
+            return 0
+
+        lax.fori_loop(1, PEERS, body, 0)
+
+    all_slots = pl.ds(0, PEERS * SLOTS)
+    all_handed = [handed(wave, all_slots) for wave in range(2)]
+
+    def weighted(tiles, i, k):
+        ids = [(2 * i + half) * BLOCKS + k for half in range(2)]
+        return [weight_ref[0, v] * tiles[recv_ref[0, v]].astype(F32) for v in ids]
+
+    def both(parts, start, stop):
+        return jnp.concatenate([parts[0][start:stop], parts[1][start:stop]], axis=0)
 
     def settle(tiles, r, own):
         def body(i, _):
-            at = rows_at(r * ROWS + i * PAIR, PAIR, 16)
-            under = rows_at(WIDTH + r * ROWS + i * PAIR, PAIR, 16)
             for k in range(BLOCKS):
                 col = pl.ds(k * COLT, COLT)
-                parts = []
-                for half in range(2):
-                    v = (2 * i + half) * BLOCKS + k
-                    tile = tiles[recv_ref[0, v]]
-                    parts.append(weight_ref[0, v] * tile.astype(F32))
-                m = jnp.concatenate([parts[0][:TR], parts[1][:TR]], axis=0)
-                h = jnp.concatenate([parts[0][TR:], parts[1][TR:]], axis=0)
-                right[at, col] = h.astype(BF16)
-                right[under, col] = m.astype(BF16)
+                parts = weighted(tiles, i, k)
+                m, h = both(parts, 0, TR), both(parts, TR, EARLY)
+                right[rows_at(HEADS + r * ROWS + i * PAIR, PAIR, 16), col] = m.astype(BF16)
+                right[rows_at((r * STRIPES + 2 * i) * HEAD, 2 * HEAD, 16), col] = h.astype(BF16)
                 if own:
                     f = cc_ref[:, k * COLT : (k + 1) * COLT]
                     first = rows_at(i * 2 * HEAD, 2 * HEAD, 16)
-                    second = rows_at(ROWS // TR * HEAD + i * 2 * REST, 2 * REST, 16)
-                    for value, place in ((m * f, k * COLT), (h * -f, WIDTH + k * COLT)):
-                        side = pl.ds(place, COLT)
-                        left[first, side] = jnp.concatenate(
-                            [value[:HEAD], value[TR : TR + HEAD]], axis=0
-                        ).astype(BF16)
-                        left[second, side] = jnp.concatenate(
-                            [value[HEAD:TR], value[TR + HEAD :]], axis=0
-                        ).astype(BF16)
+                    second = rows_at(STRIPES * HEAD + i * 2 * REST, 2 * REST, 16)
+                    plain[first, col] = (both(parts, 0, HEAD) * f).astype(BF16)
+                    plain[second, col] = (both(parts, HEAD, TR) * f).astype(BF16)
+                    left[first, pl.ds(HEADS + k * COLT, COLT)] = (h * -f).astype(BF16)
             return 0
 
         lax.fori_loop(0, PAIRS, body, 0)
 
+    def settle_late(tiles, r, own):
+        def body(i, _):
+            for k in range(BLOCKS):
+                h = both(weighted(tiles, i, k), 0, REST)
+                at = rows_at(LATE + (r * STRIPES + 2 * i) * REST, 2 * REST, 16)
+                right[at, pl.ds(k * COLT, COLT)] = h.astype(BF16)
+                if own:
+                    f = cc_ref[:, k * COLT : (k + 1) * COLT]
+                    second = rows_at(STRIPES * HEAD + i * 2 * REST, 2 * REST, 16)
+                    left[second, pl.ds(HEADS + k * COLT, COLT)] = (h * -f).astype(BF16)
+            return 0
+
+        lax.fori_loop(0, PAIRS, body, 0)
+
+    def product(rows, depth, size, cross, add):
+        part = jnp.dot(left[rows, depth], right[depth, :], preferred_element_type=F32)
+        for a in range(STRIPES):
+            for k in range(BLOCKS):
+                block = part[a * size : (a + 1) * size, k * COLT : (k + 1) * COLT]
+                tile = a * BLOCKS + k
+                cross[tile] = cross[tile] + block if add else block
+
+    head_rows = slice(0, STRIPES * HEAD)
+    rest_rows = slice(STRIPES * HEAD, ROWS)
+
+    hand_on(0)
     settle(near, row, True)
-
-    all_handed = pltpu.make_async_remote_copy(
-        near, far, hand_sem, take_sem, device_id={"row": other}, device_id_type=MESH
-    )
-    all_handed.wait_recv()
+    all_handed[0].wait_recv()
     settle(far, other, False)
-
-    def product(start, size, cross):
-        rows = left[start : start + size * (ROWS // TR), :]
-        part = jnp.dot(rows, right[...], preferred_element_type=F32)
-        for a in range(ROWS // TR):
-            for k in range(BLOCKS):
-                cross[a * BLOCKS + k] = part[a * size : (a + 1) * size, k * COLT : (k + 1) * COLT]
+    ordered = jnp.dot(plain[...], perm[...], preferred_element_type=F32).astype(BF16)
+    left[:, :HEADS] = ordered[:, :HEADS]
+    left[:, LATE:] = ordered[:, HEADS:]
+    product(head_rows, slice(0, LATE), HEAD, cross_a, False)
+    product(rest_rows, slice(0, HEADS), REST, cross_b, False)
+
+    hand_on(1)
+    settle_late(near_late, row, True)
+    all_handed[1].wait_recv()
+    settle_late(far_late, other, False)
 
     def pick_back(to, cross, tsend):
         for l in range(SLOTS):
@@ -281,10 +329,13 @@
             tsend[slot] = (weight_ref[0, v] * cross[v]).astype(BF16)
 
     mine_at = pl.ds(me * SLOTS, SLOTS)
-    parts_back = ((0, HEAD, cross_a, tsend_a, trecv_a), (ROWS // TR * HEAD, REST, cross_b, tsend_b, trecv_b))
+    parts_back = (
+        (head_rows, slice(LATE, 2 * WIDTH), HEAD, cross_a, tsend_a, trecv_a),
+        (rest_rows, slice(HEADS, 2 * WIDTH), REST, cross_b, tsend_b, trecv_b),
+    )
     homes = []
-    for n, (start, size, cross, tsend, trecv) in enumerate(parts_back):
-        product(start, size, cross)
+    for n, (rows, depth, size, cross, tsend, trecv) in enumerate(parts_back):
+        product(rows, depth, size, cross, True)
 
         def send_back(step, _):
             to = spin(me, step, 1)
@@ -306,38 +357,55 @@
             tsend.at[others], trecv.at[others], bsend_sem.at[n], brecv_sem.at[n],
             device_id={"row": other}, device_id_type=MESH,
         )
-        for n, (_, _, _, tsend, trecv) in enumerate(parts_back)
+        for n, (_, _, _, _, tsend, trecv) in enumerate(parts_back)
     ]
-    for n in range(2):
-        homes[n].wait()
-        all_back[n].wait_recv()
-
     def out_copy(i):
         at = rows_at(i * PAIR, PAIR, 16)
         return pltpu.make_async_copy(gen_v.at[at], flow_out.at[0, at], out_sem.at[i])
 
+    def tile_back(trecv, i, half, k):
+        u = (2 * i + half) * BLOCKS + k
+        return trecv[inv_s[1, lax.div(u, COLT), lax.rem(u, COLT)]].astype(F32)
+
+    def add_heads(i, _):
+        for k in range(BLOCKS):
+            mask = live(i, k)
+            for half in range(2):
+                at = rows_at(k * ROWS + i * PAIR + half * TR, HEAD, 8)
+                keep = mask[half * TR : half * TR + HEAD]
+                base[at, :] += jnp.where(keep, tile_back(trecv_a, i, half, k), 0.0)
+        return 0
+
     def finish(i, _):
         at = rows_at(i * PAIR, PAIR, 16)
         for k in range(BLOCKS):
-            parts = []
+            mask = live(i, k)
+            pieces = []
             for half in range(2):
-                u = (2 * i + half) * BLOCKS + k
-                slot = inv_s[1, lax.div(u, COLT), lax.rem(u, COLT)]
-                parts += [trecv_a[slot].astype(F32), trecv_b[slot].astype(F32)]
-            back_part = jnp.where(live(i, k), jnp.concatenate(parts, axis=0), 0.0)
-            total = base[rows_at(k * ROWS + i * PAIR, PAIR, 8), :] + back_part
-            gen_v[at, pl.ds(k * COLT, COLT)] = total.astype(BF16)
+                start = k * ROWS + i * PAIR + half * TR
+                keep = mask[half * TR + HEAD : (half + 1) * TR]
+                pieces.append(base[rows_at(start, HEAD, 8), :])
+                pieces.append(
+                    base[rows_at(start + HEAD, REST, 8), :]
+                    + jnp.where(keep, tile_back(trecv_b, i, half, k), 0.0)
+                )
+            gen_v[at, pl.ds(k * COLT, COLT)] = jnp.concatenate(pieces, axis=0).astype(BF16)
         out_copy(i).start()
         return 0
 
+    homes[0].wait()
+    all_back[0].wait_recv()
+    lax.fori_loop(0, PAIRS, add_heads, 0)
+    homes[1].wait()
+    all_back[1].wait_recv()
     lax.fori_loop(0, PAIRS, finish, 0)
 
-    pltpu.make_async_remote_copy(
-        sbuf.at[others], near.at[others], send_sem, recv_sem.at[0],
-        device_id={"row": other}, device_id_type=MESH,
-    ).wait_send()
-    all_handed.wait_send()
-    for n in range(2):
+    for n, (_, out, held, _) in enumerate(waves):
+        pltpu.make_async_remote_copy(
+            out.at[others], held.at[others], send_sem.at[n], recv_sem.at[n, 0],
+            device_id={"row": other}, device_id_type=MESH,
+        ).wait_send()
+        all_handed[n].wait_send()
         all_back[n].wait_send()
     for i in range(PAIRS):
         out_copy(i).wait()
@@ -365,12 +433,18 @@
             pltpu.VMEM((ROWS, WIDTH), BF16),
             pltpu.VMEM((ROWS, WIDTH), BF16),
             pltpu.VMEM((ROWS, WIDTH), BF16),
-            pltpu.VMEM((TILES, PAIR, COLT), BF16),
-            pltpu.VMEM((PEERS * SLOTS, PAIR, COLT), BF16),
-            pltpu.VMEM((PEERS * SLOTS, PAIR, COLT), BF16),
-            pltpu.VMEM((PEERS * SLOTS, PAIR, COLT), BF16),
+            pltpu.VMEM((TILES, EARLY, COLT), BF16),
+            pltpu.VMEM((TILES, REST, COLT), BF16),
+            pltpu.VMEM((PEERS * SLOTS, EARLY, COLT), BF16),
+            pltpu.VMEM((PEERS * SLOTS, REST, COLT), BF16),
+            pltpu.VMEM((PEERS * SLOTS, EARLY, COLT), BF16),
+            pltpu.VMEM((PEERS * SLOTS, REST, COLT), BF16),
+            pltpu.VMEM((PEERS * SLOTS, EARLY, COLT), BF16),
+            pltpu.VMEM((PEERS * SLOTS, REST, COLT), BF16),
             pltpu.VMEM((2 * WIDTH, WIDTH), BF16),
             pltpu.VMEM((ROWS, 2 * WIDTH), BF16),
+            pltpu.VMEM((ROWS, WIDTH), BF16),
+            pltpu.VMEM((WIDTH, WIDTH), BF16),
             pltpu.VMEM((BLOCKS * ROWS, COLT), F32),
             pltpu.VMEM((TILES, HEAD, COLT), F32),
             pltpu.VMEM((TILES, REST, COLT), F32),
@@ -380,14 +454,14 @@
             pltpu.VMEM((PEERS * SLOTS, REST, COLT), BF16),
             pltpu.VMEM((2, 8, COLT), jnp.int32),
             pltpu.SMEM((2, 8, COLT), jnp.int32),
-            dma((3, PAIRS)),
+            dma((3, LOADS)),
             dma,
             dma((PAIRS,)),
-            dma,
-            dma,
-            dma((PEERS,)),
-            dma,
-            dma,
+            dma((2,)),
+            dma((2,)),
+            dma((2, PEERS)),
+            dma((2,)),
+            dma((2,)),
             dma((2,)),
             dma((2,)),
             dma((2,)),

time: 93.9 us -> 95.9 us (1.021); the launches traced: 93.3 us -> 94.2 us
  no operation moved by 1% of the time
where the time goes in v5:
time: 95.9 us; the launch traced here: 94.2 us
  Pallas kernels  90 us (94%)
  other arithmetic  1.65 us (2%)
  between operations  1.33 us (1%)
  local copies, waits for them, and re-layouts  1.18 us (1%)
    pallas_call x1, Pallas kernels, per_device(): pl.pallas_call(kernel, out_shape=strip, in_specs=[hbm] * 3 + [pl.BlockSpe...  90 us

profile of v5, /device:TPU:0, one launch (start us, length us, event | category | flops | bytes accessed | tf_op | source)
XLA Modules:
  0.0 94.2 jit_solution(11737757355223659184)
XLA Ops:
  1.3 0.0 copy-start
  1.3 0.0 copy-start.1
  1.3 90.0 %shard_map.113 = bf16[1,640,1280]{2,1,0:T(8,128)(2,1)} custom-call(bf16[1,640,1280]{2,1,0:T(8,128)(2,1)} %gen.1, bf16[1,640,1280]{2,1,0:T(8,128)(2,1)} %mag.1, bf16[1,640,1280]{2,1,0:T(8,128)(2,1)} %ham.1, s32[1]{0:T(128)S(6)} %copy.13.slot_ref, s32[64]{0:T(128)} %dims_in.1, f32[64,1280]{1,0:T(8,128)} %pp_in.1, f32[1,1280]{1,0:T(1,128)} %cc_in.1, ...), custom_call_target="tpu_custom_call" | custom-call | tf_op jit(solution)/shard_map/pallas_call | solution.py:420
  91.4 0.0 copy-done
  91.4 0.0 copy-done.1
  91.4 0.0 copy-start.2
  91.4 1.7 %add_convert_fusion = bf16[1,640,1280]{2,1,0:T(8,128)(2,1)} fusion(bf16[1,640,1280]{2,1,0:T(8,128)(2,1)S(1)} %copy-done, bf16[1,640,1280]{2,1,0:T(8,128)(2,1)S(1)} %copy-done.1), kind=kLoop, calls=%fused_computation | loop fusion | flops 4096000 | bytes 4915200 | tf_op jit(solution)/shard_map/convert_element_type | solution.py:416
  93.0 0.0 copy-done.2
  93.0 1.2 %copy.14 = bf16[1,640,1280]{2,1,0:T(8,128)(2,1)} copy(bf16[1,640,1280]{2,1,0:T(8,128)(2,1)S(1)} %copy-done.2) | data formatting | bytes 3276800
Async XLA Ops:
  1.3 90.1 %copy-start = (bf16[1,640,1280]{2,1,0:T(8,128)(2,1)S(1)}, bf16[1,640,1280]{2,1,0:T(8,128)(2,1)}, u32[]{:S(2)}) copy-start(bf16[1,640,1280]{2,1,0:T(8,128)(2,1)} %gen.1) | copy-start | bytes 4915204
  1.3 90.1 %copy-start.1 = (bf16[1,640,1280]{2,1,0:T(8,128)(2,1)S(1)}, bf16[1,640,1280]{2,1,0:T(8,128)(2,1)}, u32[]{:S(2)}) copy-start(bf16[1,640,1280]{2,1,0:T(8,128)(2,1)} %mag.1) | copy-start | bytes 4915204
  91.4 1.7 %copy-start.2 = (bf16[1,640,1280]{2,1,0:T(8,128)(2,1)S(1)}, bf16[1,640,1280]{2,1,0:T(8,128)(2,1)}, u32[]{:S(2)}) copy-start(bf16[1,640,1280]{2,1,0:T(8,128)(2,1)} %shard_map.113) | copy-start | bytes 4915204

commit v6 on v4

--- a/solution.py
+++ b/solution.py
@@ -24,6 +24,7 @@
 TILES = (ROWS // TR) * BLOCKS
 HEAD = 16
 REST = TR - HEAD
+LOADS = 4
 PAIR = 2 * TR
 
 
@@ -41,25 +42,25 @@
 
 def kernel(
     gen, mag, ham, slot_ref, dims_in, pp_in, cc_in, send_in, recv_in, weight_in,
-    flow_out,
+    new_out, flow_out,
     dims_ref, pp_v, cc_ref, send_ref, recv_ref, weight_ref, small_sem,
     gen_v, mag_v, ham_v, stack, sbuf, near, far, right, left, base, cross_a, cross_b, tsend_a, tsend_b, trecv_a, trecv_b,
     inv_v, inv_s,
-    in_sem, inv_sem, out_sem, self_sem, send_sem, recv_sem, hand_sem, take_sem,
+    in_sem, inv_sem, self_sem, send_sem, recv_sem, hand_sem, take_sem,
     strip_send, strip_recv, bsend_sem, brecv_sem, bself_sem,
 ):
     me = lax.axis_index("chan")
     row = lax.axis_index("row")
     other = 1 - row
 
-    def load(i, start):
+    def load(part, start):
         for n, (src, dst) in enumerate(((gen, gen_v), (mag, mag_v), (ham, ham_v))):
-            at = rows_at(i * PAIR, PAIR, 16)
-            copy = pltpu.make_async_copy(src.at[0, at], dst.at[at], in_sem.at[n, i])
+            at = rows_at(part * (ROWS // LOADS), ROWS // LOADS, 16)
+            copy = pltpu.make_async_copy(src.at[0, at], dst.at[at], in_sem.at[n, part])
             copy.start() if start else copy.wait()
 
-    for i in range(PAIRS):
-        load(i, True)
+    for part in range(LOADS):
+        load(part, True)
     small = [
         pltpu.make_async_copy(src, dst, small_sem.at[n])
         for n, (src, dst) in enumerate(
@@ -95,23 +96,27 @@
         col_ids = k * COLT + lax.broadcasted_iota(jnp.int32, (1, COLT), 1)
         return row_ids < jnp.where(col_ids < limit, limit, 0)
 
-    def prologue(i, _):
-        load(i, False)
+    def cut(i):
         at = rows_at(i * PAIR, PAIR, 16)
         for k in range(BLOCKS):
             col = pl.ds(k * COLT, COLT)
             new = (mag_v[at, col].astype(F32) + STEP_SIZE * gen_v[at, col].astype(F32)).astype(BF16)
-            mag_v[at, col] = new
+            new_out[0, at, col] = new
             mask = live(i, k)
             m = jnp.where(mask, new.astype(F32), 0.0)
             h = jnp.where(mask, ham_v[at, col].astype(F32), 0.0)
-            for half in range(2):
-                cut = slice(half * TR, (half + 1) * TR)
-                tile = (2 * i + half) * BLOCKS + k
-                stack[tile] = jnp.concatenate([m[cut], h[cut]], axis=0).astype(BF16)
-        return 0
-
-    lax.fori_loop(0, PAIRS, prologue, 0)
+            for top in (0, TR):
+                stack[(2 * i + top // TR) * BLOCKS + k] = jnp.concatenate(
+                    [m[top : top + TR], h[top : top + TR]], axis=0
+                ).astype(BF16)
+
+    def prologue(part, _):
+        load(part, False)
+        for sub in range(PAIRS // LOADS):
+            cut(part * (PAIRS // LOADS) + sub)
+        return 0
+
+    lax.fori_loop(0, LOADS, prologue, 0)
     pl.semaphore_wait(barrier, PEERS)
 
     def pick(to):
@@ -170,7 +175,7 @@
         for k in range(BLOCKS):
             col = pl.ds(k * COLT, COLT)
             mask = live(i, k)
-            m = jnp.where(mask, mag_v[at, col].astype(F32), 0.0)
+            m = jnp.where(mask, new_out[0, at, col].astype(F32), 0.0)
             h = jnp.where(mask, ham_v[at, col].astype(F32), 0.0)
             f = factor[:, k * COLT : (k + 1) * COLT]
             right[rows_at(row * ROWS + i * PAIR, PAIR, 16), col] = h.astype(BF16)
@@ -308,28 +313,40 @@
         )
         for n, (_, _, _, tsend, trecv) in enumerate(parts_back)
     ]
-    for n in range(2):
-        homes[n].wait()
-        all_back[n].wait_recv()
-
-    def out_copy(i):
-        at = rows_at(i * PAIR, PAIR, 16)
-        return pltpu.make_async_copy(gen_v.at[at], flow_out.at[0, at], out_sem.at[i])
+    def tile_back(trecv, i, half, k):
+        u = (2 * i + half) * BLOCKS + k
+        return trecv[inv_s[1, lax.div(u, COLT), lax.rem(u, COLT)]].astype(F32)
+
+    def add_heads(i, _):
+        for k in range(BLOCKS):
+            mask = live(i, k)
+            for half in range(2):
+                at = rows_at(k * ROWS + i * PAIR + half * TR, HEAD, 8)
+                keep = mask[half * TR : half * TR + HEAD]
+                base[at, :] += jnp.where(keep, tile_back(trecv_a, i, half, k), 0.0)
+        return 0
 
     def finish(i, _):
         at = rows_at(i * PAIR, PAIR, 16)
         for k in range(BLOCKS):
-            parts = []
+            mask = live(i, k)
+            pieces = []
             for half in range(2):
-                u = (2 * i + half) * BLOCKS + k
-                slot = inv_s[1, lax.div(u, COLT), lax.rem(u, COLT)]
-                parts += [trecv_a[slot].astype(F32), trecv_b[slot].astype(F32)]
-            back_part = jnp.where(live(i, k), jnp.concatenate(parts, axis=0), 0.0)
-            total = base[rows_at(k * ROWS + i * PAIR, PAIR, 8), :] + back_part
-            gen_v[at, pl.ds(k * COLT, COLT)] = total.astype(BF16)
-        out_copy(i).start()
-        return 0
-
+                start = k * ROWS + i * PAIR + half * TR
+                keep = mask[half * TR + HEAD : (half + 1) * TR]
+                pieces.append(base[rows_at(start, HEAD, 8), :])
+                pieces.append(
+                    base[rows_at(start + HEAD, REST, 8), :]
+                    + jnp.where(keep, tile_back(trecv_b, i, half, k), 0.0)
+                )
+            flow_out[0, at, pl.ds(k * COLT, COLT)] = jnp.concatenate(pieces, axis=0).astype(BF16)
+        return 0
+
+    homes[0].wait()
+    all_back[0].wait_recv()
+    lax.fori_loop(0, PAIRS, add_heads, 0)
+    homes[1].wait()
+    all_back[1].wait_recv()
     lax.fori_loop(0, PAIRS, finish, 0)
 
     pltpu.make_async_remote_copy(
@@ -339,21 +356,30 @@
     all_handed.wait_send()
     for n in range(2):
         all_back[n].wait_send()
-    for i in range(PAIRS):
-        out_copy(i).wait()
+
+
+def write_out(new, flow, new_out, flow_out, sem):
+    copies = []
+    for n, (src, dst) in enumerate(((new, new_out), (flow, flow_out))):
+        for part in range(LOADS):
+            at = pl.ds(part * (ROWS // LOADS), ROWS // LOADS)
+            copies.append(pltpu.make_async_copy(src.at[0, at], dst.at[0, at], sem.at[n, part]))
+    for copy in copies:
+        copy.start()
+    for copy in copies:
+        copy.wait()
 
 
 def per_device(gen, mag, ham, slot, dims, pp, cc, send, recv, weight):
-    strip = jax.ShapeDtypeStruct(gen.shape, BF16)
-    magnus_new = (mag.astype(F32) + STEP_SIZE * gen.astype(F32)).astype(BF16)
     args = (gen, mag, ham, slot, dims, pp, cc, send.transpose(2, 0, 1), recv, weight)
     hbm = pl.BlockSpec(memory_space=pltpu.HBM)
+    vmem = pl.BlockSpec(memory_space=pltpu.VMEM)
     dma = pltpu.SemaphoreType.DMA
-    flowed = pl.pallas_call(
+    held = pl.pallas_call(
         kernel,
-        out_shape=strip,
+        out_shape=(pltpu.VMEM(gen.shape, BF16),) * 2,
         in_specs=[hbm] * 3 + [pl.BlockSpec(memory_space=pltpu.SMEM)] + [hbm] * 6,
-        out_specs=hbm,
+        out_specs=(vmem, vmem),
         scratch_shapes=[
             pltpu.SMEM(dims.shape, jnp.int32),
             pltpu.VMEM(pp.shape, F32),
@@ -380,9 +406,8 @@
             pltpu.VMEM((PEERS * SLOTS, REST, COLT), BF16),
             pltpu.VMEM((2, 8, COLT), jnp.int32),
             pltpu.SMEM((2, 8, COLT), jnp.int32),
-            dma((3, PAIRS)),
+            dma((3, LOADS)),
             dma,
-            dma((PAIRS,)),
             dma,
             dma,
             dma((PEERS,)),
@@ -395,10 +420,17 @@
             dma((2,)),
         ],
         compiler_params=pltpu.CompilerParams(
-            collective_id=0, has_side_effects=True, vmem_limit_bytes=58 << 20
+            collective_id=0, has_side_effects=True, vmem_limit_bytes=54 << 20
         ),
     )(*args)
-    return magnus_new, flowed
+    strip = jax.ShapeDtypeStruct(gen.shape, BF16)
+    return pl.pallas_call(
+        write_out,
+        out_shape=(strip, strip),
+        in_specs=[vmem, vmem],
+        out_specs=(hbm, hbm),
+        scratch_shapes=[dma((2, LOADS))],
+    )(*held)
 
 
 def solution(mesh):

time: 93.9 us -> 96.1 us (1.023)
  Pallas kernels: 89.2 us -> 91.9 us
  other arithmetic: 1.65 us -> 0 us
  local copies, waits for them, and re-layouts: 1.18 us -> 2.34 us
    pallas_call x1 -> x2, Pallas kernels: 89.2 us -> 91.9 us  [the longest x1 88.2 us: per_device(): pl.pallas_call(kernel, out_shape=(pltpu.VMEM(gen.shape, BF16),) * 2, in_s...]
    convert_element_type x1 -> x0, other arithmetic: 1.65 us -> none  [per_device(): magnus_new = (mag.astype(F32) + STEP_SIZE * gen.astype(F32)).astype(BF16)]
    unnamed x7 -> x4, local copies, waits for them, and re-layouts: 1.18 us -> 2.34 us
where the time goes in v6:
time: 96.1 us; the launch traced here: 95.6 us
  Pallas kernels  91.9 us (96%)
  local copies, waits for them, and re-layouts  2.34 us (2%)
  between operations  1.3 us (1%)
    pallas_call x1, Pallas kernels, per_device(): pl.pallas_call(kernel, out_shape=(pltpu.VMEM(gen.shape, BF16),) * 2, in_s...  88.2 us
    pallas_call x1, Pallas kernels, per_device(): pl.pallas_call(write_out, out_shape=(strip, strip), in_specs=[vmem, vmem]...  3.69 us
    unnamed x4, local copies, waits for them, and re-layouts  2.34 us

profile of v6, /device:TPU:0, one launch (start us, length us, event | category | flops | bytes accessed | tf_op | source)
XLA Modules:
  0.0 95.6 jit_solution(8063087269698953106)
XLA Ops:
  1.3 88.2 %shard_map.113 = (bf16[1,640,1280]{2,1,0:T(8,128)(2,1)S(1)}, bf16[1,640,1280]{2,1,0:T(8,128)(2,1)S(1)}) custom-call(bf16[1,640,1280]{2,1,0:T(8,128)(2,1)} %gen.1, bf16[1,640,1280]{2,1,0:T(8,128)(2,1)} %mag.1, bf16[1,640,1280]{2,1,0:T(8,128)(2,1)} %ham.1, s32[1]{0:T(128)S(6)} %copy.12.slot_ref, s32[64]{0:T(128)} %dims_in.1, f32[64,1280]{1,0:T(8,128)} %pp_in.1, ...), custom_call_target="tpu_custom_call" | custom-call | tf_op jit(solution)/shard_map/pallas_call | solution.py:378
  89.5 0.0 copy-start
  89.5 1.2 %copy-done = bf16[1,640,1280]{2,1,0:T(8,128)(2,1)} copy-done((bf16[1,640,1280]{2,1,0:T(8,128)(2,1)}, bf16[1,640,1280]{2,1,0:T(8,128)(2,1)S(1)}, u32[]{:S(2)}) %copy-start) | copy-done | bytes 1638424
  90.7 0.0 copy-start.1
  90.7 1.2 %copy-done.1 = bf16[1,640,1280]{2,1,0:T(8,128)(2,1)} copy-done((bf16[1,640,1280]{2,1,0:T(8,128)(2,1)}, bf16[1,640,1280]{2,1,0:T(8,128)(2,1)S(1)}, u32[]{:S(2)}) %copy-start.1) | copy-done | bytes 1638424
  91.9 3.7 %shard_map.114 = (bf16[1,640,1280]{2,1,0:T(8,128)(2,1)}, bf16[1,640,1280]{2,1,0:T(8,128)(2,1)}) custom-call(bf16[1,640,1280]{2,1,0:T(8,128)(2,1)} %copy-done, bf16[1,640,1280]{2,1,0:T(8,128)(2,1)} %copy-done.1), custom_call_target="tpu_custom_call" | custom-call | tf_op jit(solution)/shard_map/pallas_call | solution.py:427
Async XLA Ops:
  89.5 1.2 %copy-start = (bf16[1,640,1280]{2,1,0:T(8,128)(2,1)}, bf16[1,640,1280]{2,1,0:T(8,128)(2,1)S(1)}, u32[]{:S(2)}) copy-start(bf16[1,640,1280]{2,1,0:T(8,128)(2,1)S(1)} %get-tuple-element.4.new) | copy-start | bytes 4915204
  90.7 1.2 %copy-start.1 = (bf16[1,640,1280]{2,1,0:T(8,128)(2,1)}, bf16[1,640,1280]{2,1,0:T(8,128)(2,1)S(1)}, u32[]{:S(2)}) copy-start(bf16[1,640,1280]{2,1,0:T(8,128)(2,1)S(1)} %get-tuple-element.5.flow) | copy-start | bytes 4915204

commit v7 on v6

--- a/solution.py
+++ b/solution.py
@@ -430,6 +430,7 @@
         in_specs=[vmem, vmem],
         out_specs=(hbm, hbm),
         scratch_shapes=[dma((2, LOADS))],
+        compiler_params=pltpu.CompilerParams(vmem_limit_bytes=6 << 20),
     )(*held)
 
 

time: 96.1 us -> 91.8 us (0.955)
  local copies, waits for them, and re-layouts: 2.34 us -> 0 us
  Pallas kernels: 91.9 us -> 90 us
    unnamed x4 -> x0, local copies, waits for them, and re-layouts: 2.34 us -> none
    pallas_call x1, Pallas kernels: 3.69 us -> 1.77 us  [per_device(): pl.pallas_call(write_out, out_shape=(strip, strip), in_specs=[vmem, vmem]...]
where the time goes in v7:
time: 91.8 us; the launch traced here: 91.3 us
  Pallas kernels  90 us (98%)
  between operations  1.29 us (1%)
    pallas_call x1, Pallas kernels, per_device(): pl.pallas_call(kernel, out_shape=(pltpu.VMEM(gen.shape, BF16),) * 2, in_s...  88.2 us

profile of v7, /device:TPU:0, one launch (start us, length us, event | category | flops | bytes accessed | tf_op | source)
XLA Modules:
  0.0 91.3 jit_solution(8222250363280847736)
XLA Ops:
  1.3 88.2 %shard_map.113 = (bf16[1,640,1280]{2,1,0:T(8,128)(2,1)S(1)}, bf16[1,640,1280]{2,1,0:T(8,128)(2,1)S(1)}) custom-call(bf16[1,640,1280]{2,1,0:T(8,128)(2,1)} %gen.1, bf16[1,640,1280]{2,1,0:T(8,128)(2,1)} %mag.1, bf16[1,640,1280]{2,1,0:T(8,128)(2,1)} %ham.1, s32[1]{0:T(128)S(6)} %copy.12.slot_ref, s32[64]{0:T(128)} %dims_in.1, f32[64,1280]{1,0:T(8,128)} %pp_in.1, ...), custom_call_target="tpu_custom_call" | custom-call | tf_op jit(solution)/shard_map/pallas_call | solution.py:378
  89.5 1.8 %shard_map.114 = (bf16[1,640,1280]{2,1,0:T(8,128)(2,1)}, bf16[1,640,1280]{2,1,0:T(8,128)(2,1)}) custom-call(bf16[1,640,1280]{2,1,0:T(8,128)(2,1)S(1)} %get-tuple-element.4.new, bf16[1,640,1280]{2,1,0:T(8,128)(2,1)S(1)} %get-tuple-element.5.flow), custom_call_target="tpu_custom_call" | custom-call | tf_op jit(solution)/shard_map/pallas_call | solution.py:427

commit v8 on v7

--- a/solution.py
+++ b/solution.py
@@ -29,10 +29,10 @@
 
 
 def spin(me, step, sign):
-    off = lax.rem(step * MULT, PEERS)
-    x = lax.rem(lax.rem(me, 4) + 4 + sign * lax.rem(off, 4), 4)
-    y = lax.rem(lax.rem(lax.div(me, 4), 4) + 4 + sign * lax.rem(lax.div(off, 4), 4), 4)
-    z = lax.rem(lax.div(me, 16) + 4 + sign * lax.div(off, 16), 4)
+    off = step * MULT % PEERS
+    x = lax.rem(lax.rem(me, 4) + (4 + sign * (off % 4)), 4)
+    y = lax.rem(lax.rem(lax.div(me, 4), 4) + (4 + sign * (off // 4 % 4)), 4)
+    z = lax.rem(lax.div(me, 16) + (4 + sign * (off // 16)), 4)
     return (z * 4 + y) * 4 + x
 
 
@@ -153,12 +153,12 @@
             device_id={"row": other}, device_id_type=MESH,
         )
 
-    def send_out(step, _):
+    def send_out(step):
         pick(spin(me, step, 1))
         message(step).start()
-        return 0
-
-    lax.fori_loop(1, PEERS, send_out, 0)
+
+    for step in range(1, PEERS):
+        send_out(step)
     pick(me)
     mine = pltpu.make_async_copy(
         sbuf.at[pl.ds(me * SLOTS, SLOTS)], near.at[pl.ds(me * SLOTS, SLOTS)], self_sem
@@ -226,12 +226,12 @@
         base[pl.ds(k * ROWS, ROWS), :] += part[:, k * COLT : (k + 1) * COLT]
     inv_copy.wait()
 
-    def hand_on(step, _):
+    def hand_on(step):
         arrival(step).wait_recv()
         handed(step).start()
-        return 0
-
-    lax.fori_loop(1, PEERS, hand_on, 0)
+
+    for step in range(1, PEERS):
+        hand_on(step)
 
     def settle(tiles, r, own):
         def body(i, _):
@@ -291,16 +291,16 @@
     for n, (start, size, cross, tsend, trecv) in enumerate(parts_back):
         product(start, size, cross)
 
-        def send_back(step, _):
+        def send_back(step):
             to = spin(me, step, 1)
             pick_back(to, cross, tsend)
             pltpu.make_async_remote_copy(
                 tsend.at[pl.ds(to * SLOTS, SLOTS)], trecv.at[mine_at], bsend_sem.at[n], brecv_sem.at[n],
                 device_id={"chan": to}, device_id_type=MESH,
             ).start()
-            return 0
-
-        lax.fori_loop(1, PEERS, send_back, 0)
+
+        for step in range(1, PEERS):
+            send_back(step)
         pick_back(me, cross, tsend)
         homes.append(pltpu.make_async_copy(tsend.at[mine_at], trecv.at[mine_at], bself_sem.at[n]))
         homes[n].start()

time: 91.8 us -> 91.1 us (level)
  no operation moved by 1% of the time
where the time goes in v8:
time: 91.1 us; the launch traced here: 90.9 us
  Pallas kernels  89.7 us (98%)
  between operations  1.29 us (1%)
    pallas_call x1, Pallas kernels, per_device(): pl.pallas_call(kernel, out_shape=(pltpu.VMEM(gen.shape, BF16),) * 2, in_s...  87.9 us

profile of v8, /device:TPU:0, one launch (start us, length us, event | category | flops | bytes accessed | tf_op | source)
XLA Modules:
  0.0 90.9 jit_solution(11022800563046596101)
XLA Ops:
  1.3 87.9 %shard_map.113 = (bf16[1,640,1280]{2,1,0:T(8,128)(2,1)S(1)}, bf16[1,640,1280]{2,1,0:T(8,128)(2,1)S(1)}) custom-call(bf16[1,640,1280]{2,1,0:T(8,128)(2,1)} %gen.1, bf16[1,640,1280]{2,1,0:T(8,128)(2,1)} %mag.1, bf16[1,640,1280]{2,1,0:T(8,128)(2,1)} %ham.1, s32[1]{0:T(128)S(6)} %copy.12.slot_ref, s32[64]{0:T(128)} %dims_in.1, f32[64,1280]{1,0:T(8,128)} %pp_in.1, ...), custom_call_target="tpu_custom_call" | custom-call | tf_op jit(solution)/shard_map/pallas_call | solution.py:378
  89.2 1.8 %shard_map.114 = (bf16[1,640,1280]{2,1,0:T(8,128)(2,1)}, bf16[1,640,1280]{2,1,0:T(8,128)(2,1)}) custom-call(bf16[1,640,1280]{2,1,0:T(8,128)(2,1)S(1)} %get-tuple-element.4.new, bf16[1,640,1280]{2,1,0:T(8,128)(2,1)S(1)} %get-tuple-element.5.flow), custom_call_target="tpu_custom_call" | custom-call | tf_op jit(solution)/shard_map/pallas_call | solution.py:427

commit v9 on v8

--- a/solution.py
+++ b/solution.py
@@ -59,8 +59,6 @@
             copy = pltpu.make_async_copy(src.at[0, at], dst.at[at], in_sem.at[n, part])
             copy.start() if start else copy.wait()
 
-    for part in range(LOADS):
-        load(part, True)
     small = [
         pltpu.make_async_copy(src, dst, small_sem.at[n])
         for n, (src, dst) in enumerate(
@@ -74,18 +72,19 @@
             )
         )
     ]
-    for copy in small:
-        copy.start()
+    load(0, True)
     barrier = pltpu.get_barrier_semaphore()
-
-    def greet(step, _):
+    pl.semaphore_signal(barrier, inc=1, device_id={"row": other}, device_id_type=MESH)
+    for step in range(1, PEERS):
         pl.semaphore_signal(
             barrier, inc=1, device_id={"chan": lax.rem(me + step, PEERS)}, device_id_type=MESH
         )
-        return 0
-
-    lax.fori_loop(1, PEERS, greet, 0)
-    pl.semaphore_signal(barrier, inc=1, device_id={"row": other}, device_id_type=MESH)
+    for copy in small[:2]:
+        copy.start()
+    for part in range(1, LOADS):
+        load(part, True)
+    for copy in small[2:]:
+        copy.start()
 
     for copy in small[:2]:
         copy.wait()

time: 91.1 us -> 90.8 us (level)
  no operation moved by 1% of the time
where the time goes in v9:
time: 90.8 us; the launch traced here: 90.7 us
  Pallas kernels  89.4 us (98%)
  between operations  1.29 us (1%)
    pallas_call x1, Pallas kernels, per_device(): pl.pallas_call(kernel, out_shape=(pltpu.VMEM(gen.shape, BF16),) * 2, in_s...  87.6 us

profile of v9, /device:TPU:0, one launch (start us, length us, event | category | flops | bytes accessed | tf_op | source)
XLA Modules:
  0.0 90.7 jit_solution(16459582073144269377)
XLA Ops:
  1.3 87.6 %shard_map.113 = (bf16[1,640,1280]{2,1,0:T(8,128)(2,1)S(1)}, bf16[1,640,1280]{2,1,0:T(8,128)(2,1)S(1)}) custom-call(bf16[1,640,1280]{2,1,0:T(8,128)(2,1)} %gen.1, bf16[1,640,1280]{2,1,0:T(8,128)(2,1)} %mag.1, bf16[1,640,1280]{2,1,0:T(8,128)(2,1)} %ham.1, s32[1]{0:T(128)S(6)} %copy.12.slot_ref, s32[64]{0:T(128)} %dims_in.1, f32[64,1280]{1,0:T(8,128)} %pp_in.1, ...), custom_call_target="tpu_custom_call" | custom-call | tf_op jit(solution)/shard_map/pallas_call | solution.py:377
  88.9 1.8 %shard_map.114 = (bf16[1,640,1280]{2,1,0:T(8,128)(2,1)}, bf16[1,640,1280]{2,1,0:T(8,128)(2,1)}) custom-call(bf16[1,640,1280]{2,1,0:T(8,128)(2,1)S(1)} %get-tuple-element.4.new, bf16[1,640,1280]{2,1,0:T(8,128)(2,1)S(1)} %get-tuple-element.5.flow), custom_call_target="tpu_custom_call" | custom-call | tf_op jit(solution)/shard_map/pallas_call | solution.py:426

commit v10 on v9

--- a/solution.py
+++ b/solution.py
@@ -44,7 +44,7 @@
     gen, mag, ham, slot_ref, dims_in, pp_in, cc_in, send_in, recv_in, weight_in,
     new_out, flow_out,
     dims_ref, pp_v, cc_ref, send_ref, recv_ref, weight_ref, small_sem,
-    gen_v, mag_v, ham_v, stack, sbuf, near, far, right, left, base, cross_a, cross_b, tsend_a, tsend_b, trecv_a, trecv_b,
+    gen_v, mag_v, ham_v, stack, sbuf, near, far, right_near, right_far, left, base, cross_a, cross_b, tsend_a, tsend_b, trecv_a, trecv_b,
     inv_v, inv_s,
     in_sem, inv_sem, self_sem, send_sem, recv_sem, hand_sem, take_sem,
     strip_send, strip_recv, bsend_sem, brecv_sem, bself_sem,
@@ -94,6 +94,12 @@
         row_ids = row * ROWS + i * PAIR + lax.broadcasted_iota(jnp.int32, (PAIR, COLT), 0)
         col_ids = k * COLT + lax.broadcasted_iota(jnp.int32, (1, COLT), 1)
         return row_ids < jnp.where(col_ids < limit, limit, 0)
+
+    def seat(which, k):
+        half = k // (BLOCKS // 2)
+        away = row if half == 0 else other
+        start = away * WIDTH + which * ROWS + (k % (BLOCKS // 2)) * COLT
+        return pl.ds(pl.multiple_of(start, COLT), COLT)
 
     def cut(i):
         at = rows_at(i * PAIR, PAIR, 16)
@@ -177,24 +183,20 @@
             m = jnp.where(mask, new_out[0, at, col].astype(F32), 0.0)
             h = jnp.where(mask, ham_v[at, col].astype(F32), 0.0)
             f = factor[:, k * COLT : (k + 1) * COLT]
-            right[rows_at(row * ROWS + i * PAIR, PAIR, 16), col] = h.astype(BF16)
-            right[rows_at(WIDTH + row * ROWS + i * PAIR, PAIR, 16), col] = m.astype(BF16)
-            left[at, col] = (m * f).astype(BF16)
-            left[at, pl.ds(WIDTH + k * COLT, COLT)] = (h * -f).astype(BF16)
+            right_near[at, col] = h.astype(BF16)
+            right_near[rows_at(ROWS + i * PAIR, PAIR, 16), col] = m.astype(BF16)
+            left[at, seat(0, k)] = (m * f).astype(BF16)
+            left[at, seat(1, k)] = (h * -f).astype(BF16)
             base[rows_at(k * ROWS + i * PAIR, PAIR, 8), :] = h
         return 0
 
     lax.fori_loop(0, PAIRS, strips, 0)
 
-    def strip(which, r):
-        at = rows_at(which * WIDTH + r * ROWS, ROWS, 16)
-        return pltpu.make_async_remote_copy(
-            right.at[at], right.at[at], strip_send.at[which], strip_recv.at[which],
-            device_id={"row": other}, device_id_type=MESH,
-        )
-
-    for which in range(2):
-        strip(which, row).start()
+    strips_over = pltpu.make_async_remote_copy(
+        right_near, right_far, strip_send, strip_recv,
+        device_id={"row": other}, device_id_type=MESH,
+    )
+    strips_over.start()
     mine.wait()
     handed(0).start()
 
@@ -216,13 +218,16 @@
     inv_copy = pltpu.make_async_copy(inv_v, inv_s, inv_sem)
     inv_copy.start()
 
-    for which in range(2):
-        strip(which, other).wait_recv()
-        strip(which, row).wait_send()
-
-    part = jnp.dot(left[...], right[...], preferred_element_type=F32)
-    for k in range(BLOCKS):
-        base[pl.ds(k * ROWS, ROWS), :] += part[:, k * COLT : (k + 1) * COLT]
+    def pp_product(half, right):
+        part = jnp.dot(left[:, half], right[...], preferred_element_type=F32)
+        for k in range(BLOCKS):
+            base[pl.ds(k * ROWS, ROWS), :] += part[:, k * COLT : (k + 1) * COLT]
+
+    near_half, far_half = slice(0, WIDTH), slice(WIDTH, 2 * WIDTH)
+    pp_product(near_half, right_near)
+    strips_over.wait_recv()
+    pp_product(far_half, right_far)
+    strips_over.wait_send()
     inv_copy.wait()
 
     def hand_on(step):
@@ -232,10 +237,10 @@
     for step in range(1, PEERS):
         hand_on(step)
 
-    def settle(tiles, r, own):
+    def settle(tiles, right, own):
         def body(i, _):
-            at = rows_at(r * ROWS + i * PAIR, PAIR, 16)
-            under = rows_at(WIDTH + r * ROWS + i * PAIR, PAIR, 16)
+            at = rows_at(i * PAIR, PAIR, 16)
+            under = rows_at(ROWS + i * PAIR, PAIR, 16)
             for k in range(BLOCKS):
                 col = pl.ds(k * COLT, COLT)
                 parts = []
@@ -251,8 +256,7 @@
                     f = cc_ref[:, k * COLT : (k + 1) * COLT]
                     first = rows_at(i * 2 * HEAD, 2 * HEAD, 16)
                     second = rows_at(ROWS // TR * HEAD + i * 2 * REST, 2 * REST, 16)
-                    for value, place in ((m * f, k * COLT), (h * -f, WIDTH + k * COLT)):
-                        side = pl.ds(place, COLT)
+                    for value, side in ((m * f, seat(0, k)), (h * -f, seat(1, k))):
                         left[first, side] = jnp.concatenate(
                             [value[:HEAD], value[TR : TR + HEAD]], axis=0
                         ).astype(BF16)
@@ -263,20 +267,22 @@
 
         lax.fori_loop(0, PAIRS, body, 0)
 
-    settle(near, row, True)
-
+    def product(part_rows, half, right, size, cross, add):
+        part = jnp.dot(left[part_rows, half], right[...], preferred_element_type=F32)
+        for a in range(ROWS // TR):
+            for k in range(BLOCKS):
+                block = part[a * size : (a + 1) * size, k * COLT : (k + 1) * COLT]
+                tile = a * BLOCKS + k
+                cross[tile] = cross[tile] + block if add else block
+
+    head_rows, rest_rows = slice(0, ROWS // TR * HEAD), slice(ROWS // TR * HEAD, ROWS)
+    settle(near, right_near, True)
+    product(head_rows, near_half, right_near, HEAD, cross_a, False)
     all_handed = pltpu.make_async_remote_copy(
         near, far, hand_sem, take_sem, device_id={"row": other}, device_id_type=MESH
     )
     all_handed.wait_recv()
-    settle(far, other, False)
-
-    def product(start, size, cross):
-        rows = left[start : start + size * (ROWS // TR), :]
-        part = jnp.dot(rows, right[...], preferred_element_type=F32)
-        for a in range(ROWS // TR):
-            for k in range(BLOCKS):
-                cross[a * BLOCKS + k] = part[a * size : (a + 1) * size, k * COLT : (k + 1) * COLT]
+    settle(far, right_far, False)
 
     def pick_back(to, cross, tsend):
         for l in range(SLOTS):
@@ -285,10 +291,15 @@
             tsend[slot] = (weight_ref[0, v] * cross[v]).astype(BF16)
 
     mine_at = pl.ds(me * SLOTS, SLOTS)
-    parts_back = ((0, HEAD, cross_a, tsend_a, trecv_a), (ROWS // TR * HEAD, REST, cross_b, tsend_b, trecv_b))
+    parts_back = (
+        (head_rows, HEAD, cross_a, tsend_a, trecv_a),
+        (rest_rows, REST, cross_b, tsend_b, trecv_b),
+    )
     homes = []
-    for n, (start, size, cross, tsend, trecv) in enumerate(parts_back):
-        product(start, size, cross)
+    for n, (part_rows, size, cross, tsend, trecv) in enumerate(parts_back):
+        if n == 1:
+            product(part_rows, near_half, right_near, size, cross, False)
+        product(part_rows, far_half, right_far, size, cross, True)
 
         def send_back(step):
             to = spin(me, step, 1)
@@ -394,7 +405,8 @@
             pltpu.VMEM((PEERS * SLOTS, PAIR, COLT), BF16),
             pltpu.VMEM((PEERS * SLOTS, PAIR, COLT), BF16),
             pltpu.VMEM((PEERS * SLOTS, PAIR, COLT), BF16),
-            pltpu.VMEM((2 * WIDTH, WIDTH), BF16),
+            pltpu.VMEM((WIDTH, WIDTH), BF16),
+            pltpu.VMEM((WIDTH, WIDTH), BF16),
             pltpu.VMEM((ROWS, 2 * WIDTH), BF16),
             pltpu.VMEM((BLOCKS * ROWS, COLT), F32),
             pltpu.VMEM((TILES, HEAD, COLT), F32),
@@ -412,8 +424,8 @@
             dma((PEERS,)),
             dma,
             dma,
-            dma((2,)),
-            dma((2,)),
+            dma,
+            dma,
             dma((2,)),
             dma((2,)),
             dma((2,)),

time: 90.8 us -> 91.7 us (level)
  no operation moved by 1% of the time
where the time goes in v10:
time: 91.7 us; the launch traced here: 91.6 us
  Pallas kernels  90.3 us (98%)
  between operations  1.29 us (1%)
    pallas_call x1, Pallas kernels, per_device(): pl.pallas_call(kernel, out_shape=(pltpu.VMEM(gen.shape, BF16),) * 2, in_s...  88.5 us

profile of v10, /device:TPU:0, one launch (start us, length us, event | category | flops | bytes accessed | tf_op | source)
XLA Modules:
  0.0 91.6 jit_solution(422540371351969841)
XLA Ops:
  1.3 88.5 %shard_map.113 = (bf16[1,640,1280]{2,1,0:T(8,128)(2,1)S(1)}, bf16[1,640,1280]{2,1,0:T(8,128)(2,1)S(1)}) custom-call(bf16[1,640,1280]{2,1,0:T(8,128)(2,1)} %gen.1, bf16[1,640,1280]{2,1,0:T(8,128)(2,1)} %mag.1, bf16[1,640,1280]{2,1,0:T(8,128)(2,1)} %ham.1, s32[1]{0:T(128)S(6)} %copy.12.slot_ref, s32[64]{0:T(128)} %dims_in.1, f32[64,1280]{1,0:T(8,128)} %pp_in.1, ...), custom_call_target="tpu_custom_call" | custom-call | tf_op jit(solution)/shard_map/pallas_call | solution.py:388
  89.8 1.8 %shard_map.114 = (bf16[1,640,1280]{2,1,0:T(8,128)(2,1)}, bf16[1,640,1280]{2,1,0:T(8,128)(2,1)}) custom-call(bf16[1,640,1280]{2,1,0:T(8,128)(2,1)S(1)} %get-tuple-element.4.new, bf16[1,640,1280]{2,1,0:T(8,128)(2,1)S(1)} %get-tuple-element.5.flow), custom_call_target="tpu_custom_call" | custom-call | tf_op jit(solution)/shard_map/pallas_call | solution.py:438

commit v11 on v9

--- a/solution.py
+++ b/solution.py
@@ -25,6 +25,7 @@
 HEAD = 16
 REST = TR - HEAD
 LOADS = 4
+BACK = 80
 PAIR = 2 * TR
 
 
@@ -44,10 +45,10 @@
     gen, mag, ham, slot_ref, dims_in, pp_in, cc_in, send_in, recv_in, weight_in,
     new_out, flow_out,
     dims_ref, pp_v, cc_ref, send_ref, recv_ref, weight_ref, small_sem,
-    gen_v, mag_v, ham_v, stack, sbuf, near, far, right, left, base, cross_a, cross_b, tsend_a, tsend_b, trecv_a, trecv_b,
+    gen_v, mag_v, ham_v, stack, sbuf, near, far, right, left, base, cross_a, cross_b, tsend_a, tsend_b, trecv_a, trecv_b, unpacked,
     inv_v, inv_s,
     in_sem, inv_sem, self_sem, send_sem, recv_sem, hand_sem, take_sem,
-    strip_send, strip_recv, bsend_sem, brecv_sem, bself_sem,
+    strip_send, strip_recv, bsend_sem, heads_sem, brecv_sem, bself_sem,
 ):
     me = lax.axis_index("chan")
     row = lax.axis_index("row")
@@ -278,43 +279,69 @@
             for k in range(BLOCKS):
                 cross[a * BLOCKS + k] = part[a * size : (a + 1) * size, k * COLT : (k + 1) * COLT]
 
-    def pick_back(to, cross, tsend):
+    def returned(to):
         for l in range(SLOTS):
             slot = to * SLOTS + l
-            v = inv_s[0, lax.div(slot, COLT), lax.rem(slot, COLT)]
-            tsend[slot] = (weight_ref[0, v] * cross[v]).astype(BF16)
-
+            yield slot, inv_s[0, lax.div(slot, COLT), lax.rem(slot, COLT)]
+
+    def pick_heads(to):
+        for slot, v in returned(to):
+            tsend_a[slot] = (weight_ref[0, v] * cross_a[v]).astype(BF16)
+
+    def pick_rests(to):
+        pieces = [weight_ref[0, v] * cross_b[v] for _, v in returned(to)]
+        pieces.append(jnp.zeros((BACK - SLOTS * REST, COLT), F32))
+        tsend_b[to] = jnp.concatenate(pieces, axis=0).astype(BF16)
+
+    def back_heads(to, place):
+        return pltpu.make_async_remote_copy(
+            tsend_a.at[pl.ds(to * SLOTS, SLOTS)], trecv_a.at[pl.ds(place * SLOTS, SLOTS)],
+            bsend_sem.at[0], heads_sem, device_id={"chan": to}, device_id_type=MESH,
+        )
+
+    def back_rests(step, to, place):
+        return pltpu.make_async_remote_copy(
+            tsend_b.at[to], trecv_b.at[place],
+            bsend_sem.at[1], brecv_sem.at[step], device_id={"chan": to}, device_id_type=MESH,
+        )
+
+    product(0, HEAD, cross_a)
+    for step in range(1, PEERS):
+        to = spin(me, step, 1)
+        pick_heads(to)
+        back_heads(to, me).start()
+    pick_heads(me)
     mine_at = pl.ds(me * SLOTS, SLOTS)
-    parts_back = ((0, HEAD, cross_a, tsend_a, trecv_a), (ROWS // TR * HEAD, REST, cross_b, tsend_b, trecv_b))
-    homes = []
-    for n, (start, size, cross, tsend, trecv) in enumerate(parts_back):
-        product(start, size, cross)
-
-        def send_back(step):
-            to = spin(me, step, 1)
-            pick_back(to, cross, tsend)
-            pltpu.make_async_remote_copy(
-                tsend.at[pl.ds(to * SLOTS, SLOTS)], trecv.at[mine_at], bsend_sem.at[n], brecv_sem.at[n],
-                device_id={"chan": to}, device_id_type=MESH,
-            ).start()
-
-        for step in range(1, PEERS):
-            send_back(step)
-        pick_back(me, cross, tsend)
-        homes.append(pltpu.make_async_copy(tsend.at[mine_at], trecv.at[mine_at], bself_sem.at[n]))
-        homes[n].start()
+    home_heads = pltpu.make_async_copy(tsend_a.at[mine_at], trecv_a.at[mine_at], bself_sem.at[0])
+    home_heads.start()
+
+    product(ROWS // TR * HEAD, REST, cross_b)
+    for step in range(1, PEERS):
+        to = spin(me, step, 1)
+        pick_rests(to)
+        back_rests(step, to, me).start()
+    pick_rests(me)
+    home_rests = pltpu.make_async_copy(tsend_b.at[me], trecv_b.at[me], bself_sem.at[1])
+    home_rests.start()
 
     others = pl.ds(0, (PEERS - 1) * SLOTS)
-    all_back = [
-        pltpu.make_async_remote_copy(
-            tsend.at[others], trecv.at[others], bsend_sem.at[n], brecv_sem.at[n],
-            device_id={"row": other}, device_id_type=MESH,
-        )
-        for n, (_, _, _, tsend, trecv) in enumerate(parts_back)
-    ]
+    all_heads = pltpu.make_async_remote_copy(
+        tsend_a.at[others], trecv_a.at[others], bsend_sem.at[0], heads_sem,
+        device_id={"row": other}, device_id_type=MESH,
+    )
+    all_rests = pltpu.make_async_remote_copy(
+        tsend_b.at[pl.ds(0, PEERS - 1)], trecv_b.at[pl.ds(0, PEERS - 1)], bsend_sem.at[1],
+        brecv_sem.at[0], device_id={"row": other}, device_id_type=MESH,
+    )
+
+    def unpack(fr):
+        rows = trecv_b[fr].astype(F32)
+        for l in range(SLOTS):
+            unpacked[fr * SLOTS + l] = rows[l * REST : (l + 1) * REST]
+
     def tile_back(trecv, i, half, k):
         u = (2 * i + half) * BLOCKS + k
-        return trecv[inv_s[1, lax.div(u, COLT), lax.rem(u, COLT)]].astype(F32)
+        return trecv[inv_s[1, lax.div(u, COLT), lax.rem(u, COLT)]]
 
     def add_heads(i, _):
         for k in range(BLOCKS):
@@ -322,7 +349,7 @@
             for half in range(2):
                 at = rows_at(k * ROWS + i * PAIR + half * TR, HEAD, 8)
                 keep = mask[half * TR : half * TR + HEAD]
-                base[at, :] += jnp.where(keep, tile_back(trecv_a, i, half, k), 0.0)
+                base[at, :] += jnp.where(keep, tile_back(trecv_a, i, half, k).astype(F32), 0.0)
         return 0
 
     def finish(i, _):
@@ -336,16 +363,20 @@
                 pieces.append(base[rows_at(start, HEAD, 8), :])
                 pieces.append(
                     base[rows_at(start + HEAD, REST, 8), :]
-                    + jnp.where(keep, tile_back(trecv_b, i, half, k), 0.0)
+                    + jnp.where(keep, tile_back(unpacked, i, half, k), 0.0)
                 )
             flow_out[0, at, pl.ds(k * COLT, COLT)] = jnp.concatenate(pieces, axis=0).astype(BF16)
         return 0
 
-    homes[0].wait()
-    all_back[0].wait_recv()
+    home_heads.wait()
+    all_heads.wait_recv()
     lax.fori_loop(0, PAIRS, add_heads, 0)
-    homes[1].wait()
-    all_back[1].wait_recv()
+    home_rests.wait()
+    unpack(me)
+    for step in range(1, PEERS):
+        fr = spin(me, step, -1)
+        back_rests(step, fr, fr).wait_recv()
+        unpack(fr)
     lax.fori_loop(0, PAIRS, finish, 0)
 
     pltpu.make_async_remote_copy(
@@ -353,8 +384,8 @@
         device_id={"row": other}, device_id_type=MESH,
     ).wait_send()
     all_handed.wait_send()
-    for n in range(2):
-        all_back[n].wait_send()
+    all_heads.wait_send()
+    all_rests.wait_send()
 
 
 def write_out(new, flow, new_out, flow_out, sem):
@@ -400,9 +431,10 @@
             pltpu.VMEM((TILES, HEAD, COLT), F32),
             pltpu.VMEM((TILES, REST, COLT), F32),
             pltpu.VMEM((PEERS * SLOTS, HEAD, COLT), BF16),
-            pltpu.VMEM((PEERS * SLOTS, REST, COLT), BF16),
+            pltpu.VMEM((PEERS, BACK, COLT), BF16),
             pltpu.VMEM((PEERS * SLOTS, HEAD, COLT), BF16),
-            pltpu.VMEM((PEERS * SLOTS, REST, COLT), BF16),
+            pltpu.VMEM((PEERS, BACK, COLT), BF16),
+            pltpu.VMEM((PEERS * SLOTS, REST, COLT), F32),
             pltpu.VMEM((2, 8, COLT), jnp.int32),
             pltpu.SMEM((2, 8, COLT), jnp.int32),
             dma((3, LOADS)),
@@ -415,7 +447,8 @@
             dma((2,)),
             dma((2,)),
             dma((2,)),
-            dma((2,)),
+            dma,
+            dma((PEERS,)),
             dma((2,)),
         ],
         compiler_params=pltpu.CompilerParams(

time: 90.8 us -> 93 us (1.024)
  Pallas kernels: 89.4 us -> 91.5 us
    pallas_call x1, Pallas kernels: 87.6 us -> 89.8 us  [per_device(): pl.pallas_call(kernel, out_shape=(pltpu.VMEM(gen.shape, BF16),) * 2, in_s...]
where the time goes in v11:
time: 93 us; the launch traced here: 92.8 us
  Pallas kernels  91.5 us (98%)
  between operations  1.29 us (1%)
    pallas_call x1, Pallas kernels, per_device(): pl.pallas_call(kernel, out_shape=(pltpu.VMEM(gen.shape, BF16),) * 2, in_s...  89.8 us

profile of v11, /device:TPU:0, one launch (start us, length us, event | category | flops | bytes accessed | tf_op | source)
XLA Modules:
  0.0 92.8 jit_solution(12749455888219415292)
XLA Ops:
  1.3 89.8 %shard_map.113 = (bf16[1,640,1280]{2,1,0:T(8,128)(2,1)S(1)}, bf16[1,640,1280]{2,1,0:T(8,128)(2,1)S(1)}) custom-call(bf16[1,640,1280]{2,1,0:T(8,128)(2,1)} %gen.1, bf16[1,640,1280]{2,1,0:T(8,128)(2,1)} %mag.1, bf16[1,640,1280]{2,1,0:T(8,128)(2,1)} %ham.1, s32[1]{0:T(128)S(6)} %copy.12.slot_ref, s32[64]{0:T(128)} %dims_in.1, f32[64,1280]{1,0:T(8,128)} %pp_in.1, ...), custom_call_target="tpu_custom_call" | custom-call | tf_op jit(solution)/shard_map/pallas_call | solution.py:408
  91.1 1.8 %shard_map.114 = (bf16[1,640,1280]{2,1,0:T(8,128)(2,1)}, bf16[1,640,1280]{2,1,0:T(8,128)(2,1)}) custom-call(bf16[1,640,1280]{2,1,0:T(8,128)(2,1)S(1)} %get-tuple-element.4.new, bf16[1,640,1280]{2,1,0:T(8,128)(2,1)S(1)} %get-tuple-element.5.flow), custom_call_target="tpu_custom_call" | custom-call | tf_op jit(solution)/shard_map/pallas_call | solution.py:459
